TPU v7x, 32 devices: a whole 2x2x4 slice. The times are simulated.
32 devices in a mesh: req: 8 (over y, x, core), kv: 4 (over z).
Axes of the slice: x: 2, y: 2, z: 4, core: 2. Of those that a mesh axis runs over, the one named last changes fastest.
Arguments:
- hidden: bfloat16 [512, 2048], P('req', 'kv'), may hold values from -6 to 6
- attn_gain: float32 [2048], replicated, may hold values from 0.25 to 1.75
- q_gain: float32 [128], replicated, may hold values from 0.25 to 1.75
- k_gain: float32 [128], replicated, may hold values from 0.25 to 1.75
- w_q: bfloat16 [2048, 2048], P(None, 'kv'), may hold values from -0.125 to 0.125
- w_gate_attn: bfloat16 [2048, 2048], P(None, 'kv'), may hold values from -0.125 to 0.125
- w_k: bfloat16 [2048, 1024], P(None, 'kv'), may hold values from -0.125 to 0.125
- w_v: bfloat16 [2048, 1024], P(None, 'kv'), may hold values from -0.125 to 0.125
- w_o: bfloat16 [2048, 2048], P('kv'), may hold values from -0.125 to 0.125
- k_pool: bfloat16 [1200, 128, 1024], P('req', None, 'kv'), may hold values from -245 to 245
- v_pool: bfloat16 [1200, 128, 1024], P('req', None, 'kv'), may hold values from -6 to 6
- lengths: int32 [512], P('req'), may hold values from 1 to 4095, as said below
- page_table: int32 [512, 32], P('req'), may hold values from 0 to 149, as said below
- mig_request: int32 [8, 8], P('req'), may hold values from 0 to 63, as said below
- mig_dest: int32 [8, 8], P('req'), may hold values from 0 to 7, as said below
- mlp_gain: float32 [2048], replicated, may hold values from 0.25 to 1.75
- w_gate: bfloat16 [2048, 6144], P(None, ('req', 'kv')), may hold values from -0.125 to 0.125
- w_up: bfloat16 [2048, 6144], P(None, ('req', 'kv')), may hold values from -0.125 to 0.125
- w_down: bfloat16 [2048, 6144], P(None, ('req', 'kv')), may hold values from -0.078125 to 0.078125
Outputs:
- out_hidden: bfloat16 [512, 2048], P('req', 'kv')
- mig_keys: bfloat16 [64, 512, 1024], P('req', None, 'kv')
- mig_values: bfloat16 [64, 512, 1024], P('req', None, 'kv')
Inputs may be any that keep to these rules, and one draw needn't show every extreme that they name: lengths[r] tokens of request r are cached and its new token takes position lengths[r]; some request holds 4095 cached tokens. `page_table`: entries refer to the pool of the request's own device. The first lengths[r] // 128 + 1 entries of row r are the request's pages, distinct and never shared with another request of that device; later entries are valid pages that are not read. `mig_request`: row s names 8 different requests of device s; each has at most 511 cached tokens, and in every row one has exactly that many. `mig_dest`: each row is a permutation.
All inputs are finite; a program needn't handle non-finite values.
Results may differ from a plain program's by a relative error of at most 0.0093.
Values may be sent and summed in bfloat16 or wider, within the bound.
A program may use at most 128 MiB of HBM per device.

v0:
```python
import jax
import jax.numpy as jnp
from jax import lax
from jax.sharding import PartitionSpec as P

MIGP = 4


EPSILON = 1e-06
ROPE_BASE = 1000000.0
SLOT_BLOCK = 4


def rms_norm(values, scale_row):
    values = values.astype(jnp.float32)
    return (
        values * lax.rsqrt(jnp.mean(values * values, axis=-1, keepdims=True) + EPSILON) * scale_row
    )


def rotate(values, position):
    half_dim = values.shape[-1] // 2
    frequency = ROPE_BASE ** (-jnp.arange(half_dim, dtype=jnp.float32) * 2.0 / values.shape[-1])
    angles = position.astype(jnp.float32)[:, None, None] * frequency
    cosine = jnp.cos(angles)
    sine_part = jnp.sin(angles)
    first_half = values[..., :half_dim]
    second = values[..., half_dim:]
    return jnp.concatenate(
        [first_half * cosine - second * sine_part, second * cosine + first_half * sine_part],
        axis=-1,
    )


def attend_slots(queries, new_keys, new_values, k_pool, v_pool, lengths, page_table):
    req_count, kv_local, group_size, head_dim = queries.shape
    page_size = k_pool.shape[1]
    slot_span = page_table.shape[1] * page_size
    score_scale = head_dim ** (-0.5)
    used_pages = jnp.max(lengths) // page_size + 1
    turn_count = (used_pages + SLOT_BLOCK - 1) // SLOT_BLOCK
    block_width = SLOT_BLOCK * page_size

    def score_block(turn_index, buffer):
        page_ids = lax.dynamic_slice_in_dim(page_table, turn_index * SLOT_BLOCK, SLOT_BLOCK, 1)
        key_block = k_pool[page_ids].reshape(req_count, block_width, kv_local, head_dim)
        scores = (
            jnp.einsum("rkgd,rtkd->rkgt", queries, key_block, preferred_element_type=jnp.float32)
            * score_scale
        )
        return lax.dynamic_update_slice_in_dim(buffer, scores, turn_index * block_width, 3)

    start_buffer = jnp.full((req_count, kv_local, group_size, slot_span), -jnp.inf, jnp.float32)
    scores = lax.fori_loop(0, turn_count, score_block, start_buffer)
    position = jnp.arange(slot_span, dtype=jnp.int32)
    scores = jnp.where(
        position[None, None, None, :] < lengths[:, None, None, None], scores, -jnp.inf
    )
    own_score = (
        jnp.einsum("rkgd,rkd->rkg", queries, new_keys, preferred_element_type=jnp.float32)
        * score_scale
    )
    row_top = jnp.maximum(jnp.max(scores, axis=-1), own_score)
    exps_all = jnp.exp(scores - row_top[..., None])
    own_exp = jnp.exp(own_score - row_top)
    denom_sum = jnp.sum(exps_all, axis=-1) + own_exp
    weights = (exps_all / denom_sum[..., None]).astype(jnp.bfloat16)
    own_weight = (own_exp / denom_sum).astype(jnp.bfloat16)

    def value_block(turn_index, context_sum):
        page_ids = lax.dynamic_slice_in_dim(page_table, turn_index * SLOT_BLOCK, SLOT_BLOCK, 1)
        val_block = v_pool[page_ids].reshape(req_count, block_width, kv_local, head_dim)
        weight_block = lax.dynamic_slice_in_dim(weights, turn_index * block_width, block_width, 3)
        return context_sum + jnp.einsum(
            "rkgt,rtkd->rkgd", weight_block, val_block, preferred_element_type=jnp.float32
        )

    start_sum = jnp.einsum(
        "rkg,rkd->rkgd", own_weight, new_values, preferred_element_type=jnp.float32
    )
    return lax.fori_loop(0, turn_count, value_block, start_sum)


def hidden_full_add(whole_rows, attn_sum):
    return whole_rows.astype(jnp.float32) + attn_sum


def per_device(
    hidden,
    attn_gain,
    q_gain,
    k_gain,
    w_q,
    w_gate_attn,
    w_k,
    w_v,
    w_o,
    k_pool,
    v_pool,
    lengths,
    page_table,
    mig_request,
    mig_dest,
    mlp_gain,
    w_gate,
    w_up,
    w_down,
):
    head_dim = q_gain.shape[0]
    req_count = hidden.shape[0]
    kv_local = w_k.shape[1] // head_dim
    q_local = w_q.shape[1] // head_dim
    group_size = q_local // kv_local
    page_size = k_pool.shape[1]
    channels = kv_local * head_dim
    model_width = mlp_gain.shape[0]
    whole_rows = lax.all_gather(hidden, "kv", axis=1, tiled=True)
    normed = rms_norm(whole_rows, attn_gain).astype(jnp.bfloat16)
    query_raw = jnp.dot(normed, w_q, preferred_element_type=jnp.float32).reshape(
        req_count, q_local, head_dim
    )
    gate_raw = jnp.dot(normed, w_gate_attn, preferred_element_type=jnp.float32)
    key_raw = jnp.dot(normed, w_k, preferred_element_type=jnp.float32).reshape(
        req_count, kv_local, head_dim
    )
    value_raw = jnp.dot(normed, w_v, preferred_element_type=jnp.float32).reshape(
        req_count, kv_local, head_dim
    )
    queries = rotate(rms_norm(query_raw, q_gain), lengths).astype(jnp.bfloat16)
    queries = queries.reshape(req_count, kv_local, group_size, head_dim)
    new_keys = rotate(rms_norm(key_raw, k_gain), lengths).astype(jnp.bfloat16)
    new_values = value_raw.astype(jnp.bfloat16)
    mig_rows = mig_request[0]
    dest_row = mig_dest[0]
    mig_count = mig_rows.shape[0]
    slot_count = MIGP * page_size
    moved_pages = page_table[mig_rows, :MIGP]
    slot_pos = jnp.arange(slot_count, dtype=jnp.int32)[None, :, None]
    moved_len = lengths[mig_rows][:, None, None]
    zero_value = jnp.zeros((), jnp.bfloat16)
    inverse = jnp.zeros_like(dest_row).at[dest_row].set(jnp.arange(mig_count, dtype=jnp.int32))

    def place_cache(pool, fresh_rows):
        cached = pool[moved_pages].reshape(mig_count, slot_count, channels)
        fresh_row = fresh_rows.reshape(req_count, channels)[mig_rows][:, None, :]
        filled = jnp.where(
            slot_pos < moved_len, cached, jnp.where(slot_pos == moved_len, fresh_row, zero_value)
        )
        return filled[inverse]

    mig_keys, mig_values = (
        lax.all_to_all(
            place_cache(k_pool, new_keys), "req", split_axis=0, concat_axis=0, tiled=True
        ),
        lax.all_to_all(
            place_cache(v_pool, new_values), "req", split_axis=0, concat_axis=0, tiled=True
        ),
    )
    context = attend_slots(queries, new_keys, new_values, k_pool, v_pool, lengths, page_table)
    gated = (jax.nn.sigmoid(gate_raw) * context.reshape(req_count, q_local * head_dim)).astype(
        jnp.bfloat16
    )
    head_terms = jnp.dot(gated, w_o, preferred_element_type=jnp.float32)
    attn_sum = lax.psum(head_terms, "kv")
    mid_stream = hidden_full_add(whole_rows, attn_sum).astype(jnp.bfloat16)
    normed_mlp = rms_norm(mid_stream, mlp_gain).astype(jnp.bfloat16)
    kv_count = lax.axis_size("kv")
    slice_width = model_width // kv_count
    slice_start = lax.axis_index("kv") * slice_width
    mid_slice = lax.dynamic_slice_in_dim(mid_stream, slice_start, slice_width, 1)
    row_piece = lax.all_gather(normed_mlp, "req", axis=0, tiled=True)
    gate_part = jnp.dot(row_piece, w_gate, preferred_element_type=jnp.float32)
    up_part = jnp.dot(row_piece, w_up, preferred_element_type=jnp.float32)
    activation = (jax.nn.silu(gate_part) * up_part).astype(jnp.bfloat16)
    req_groups = lax.axis_size("req")
    unit_count = activation.shape[1]
    grouped_act = activation.reshape(req_groups, req_count, unit_count)
    grouped_down = w_down.reshape(kv_count, slice_width, unit_count)
    term = jnp.einsum(
        "gru,hcu->ghrc", grouped_act, grouped_down, preferred_element_type=jnp.float32
    )
    term = term.reshape(req_groups * kv_count, req_count, slice_width)
    mlp_part = lax.psum_scatter(term, ("req", "kv"), scatter_dimension=0, tiled=True)[0]
    out_hidden = (mid_slice.astype(jnp.float32) + mlp_part).astype(jnp.bfloat16)
    return (out_hidden, mig_keys, mig_values)


def solution(mesh):
    return jax.shard_map(
        per_device,
        mesh=mesh,
        in_specs=(
            P("req", "kv"),
            P(),
            P(),
            P(),
            P(None, "kv"),
            P(None, "kv"),
            P(None, "kv"),
            P(None, "kv"),
            P("kv", None),
            P("req", None, "kv"),
            P("req", None, "kv"),
            P("req"),
            P("req", None),
            P("req", None),
            P("req", None),
            P(),
            P(None, ("req", "kv")),
            P(None, ("req", "kv")),
            P(None, ("req", "kv")),
        ),
        out_specs=(P("req", "kv"), P("req", None, "kv"), P("req", None, "kv")),
        check_vma=False,
    )
```

profile of v0, /device:TPU:0, one launch (start us, length us, event | category | flops | bytes accessed | tf_op | source)
XLA Modules:
  0.0 1038.8 jit_solution(1519188205715549480)
XLA Ops:
  12.9 15.8 %all_gather.6 = bf16[64,2048]{1,0:T(8,128)(2,1)S(1)} all-gather(bf16[64,512]{1,0:T(8,128)(2,1)} %param.23), channel_id=1, replica_groups=mesh['req'=8,'kv'=4] {'kv'}, dimensions={1}, use_global_device_ids=true | all-gather | bytes 327680 | tf_op jit(solution)/shard_map/all_gather | solution.py:117
  33.2 4.2 broadcast_in_dim.61
  37.4 46.3 %while.20 = (s32[]{:T(128)}, f32[64,2,2,4096]{3,2,1,0:T(2,128)}, s32[]{:T(128)}, s32[64,32]{1,0:T(8,128)S(1)}, bf16[150,128,256]{2,1,0:T(8,128)(2,1)}, /*index=5...) while((s32[]{:T(128)}, f32[64,2,2,4096]{3,2,1,0:T(2,128)}, ...), condition=%wide.region_5.6_spmd, body=%wide.region_4.5_spmd.sunk | while | flops 33687304 | bytes 84486360 | solution.py:54
  37.6 13.6 %gather_fusion = bf16[256,128,256]{2,1,0:T(8,128)(2,1)} fusion(bf16[150,128,256]{2,1,0:T(8,128)(2,1)} %get-tuple-element.261, s32[1024]{0:T(1024)S(1)} %pad_clamp_fusion.7), kind=kCustom, calls=%fused_computation.clone.1 | custom fusion | bytes 33555456 | tf_op jit(solution)/shard_map/while/body/gather | solution.py:46
  51.1 23.7 %reshape.434 = bf16[64,512,2,128]{3,2,1,0:T(2,128)(2,1)} reshape(bf16[256,128,256]{2,1,0:T(8,128)(2,1)} %gather_fusion) | data formatting | bytes 33554432 | tf_op jit(solution)/shard_map/while/body/reshape | solution.py:46
  74.8 8.8 fusion.79
  83.7 5.2 fusion.18
  91.8 6.1 fusion.26
  98.1 6.9 divide_convert_fusion
  106.9 45.9 %while.21 = (s32[]{:T(128)}, f32[64,2,2,128]{3,2,1,0:T(2,128)S(1)}, s32[]{:T(128)}, bf16[64,2,2,4096]{3,2,1,0:T(2,128)(2,1)}, s32[64,32]{1,0:T(8,128)S(1)}, /*in...) while((s32[]{:T(128)}, f32[64,2,2,128]{3,2,1,0:T(2,128)S(1)}, ...), condition=%wide.region_9.10_spmd, body=%wide.region_8.9_spmd.sunk | while | flops 33589000 | bytes 84420824 | solution.py:81
  107.2 13.6 %gather_fusion.1 = bf16[256,128,256]{2,1,0:T(8,128)(2,1)} fusion(bf16[150,128,256]{2,1,0:T(8,128)(2,1)} %get-tuple-element.298, s32[1024]{0:T(1024)S(1)} %pad_clamp_fusion.8), kind=kCustom, calls=%fused_computation.1.clone.1 | custom fusion | bytes 33555456 | tf_op jit(solution)/shard_map/while/body/gather | solution.py:72
  120.7 23.7 %reshape.438 = bf16[64,512,2,128]{3,2,1,0:T(2,128)(2,1)} reshape(bf16[256,128,256]{2,1,0:T(8,128)(2,1)} %gather_fusion.1) | data formatting | bytes 33554432 | tf_op jit(solution)/shard_map/while/body/reshape | solution.py:72
  144.5 8.3 fusion.82
  156.6 679.8 %all-reduce.3.cloned.1.call-done = f32[64,2048]{1,0:T(8,128)} async-done(((f32[64,2048]{1,0:T(8,128)}), f32[64,2048]{1,0:T(8,128)}) %all-reduce.3.cloned.1.call-update) | async-done | bytes 524304 | tf_op jit(solution)/shard_map/psum | solution.py:164
  838.6 28.2 %all-gather.2.cloned.1.call-done = bf16[512,2048]{1,0:T(8,128)(2,1)} async-done(((bf16[64,2048]{1,0:T(8,128)(2,1)}), bf16[512,2048]{1,0:T(8,128)(2,1)}) %all-gather.2.cloned.1.call-update) | async-done | bytes 2097168 | tf_op jit(solution)/shard_map/all_gather | solution.py:171
  879.6 5.9 gather_fusion.3
  885.5 5.8 gather_fusion.6
  894.0 5.2 bitcast_select_fusion
  899.2 3.6 gather_fusion.5
  902.9 4.4 all-to-all-start
  910.8 26.9 %all-to-all-done = bf16[8,512,256]{2,1,0:T(8,128)(2,1)} async-done(((bf16[8,512,256]{2,1,0:T(8,128)(2,1)}), bf16[8,512,256]{2,1,0:T(8,128)(2,1)}, u32[]{:S(2)}, u32[]{:S(2)}) %all-to-all-start) | async-done | bytes 2097184 | tf_op jit(solution)/shard_map/all_to_all | solution.py:152
  937.8 4.4 all-to-all-start.1
  942.1 30.6 %all-to-all-done.1 = bf16[8,512,256]{2,1,0:T(8,128)(2,1)} async-done(((bf16[8,512,256]{2,1,0:T(8,128)(2,1)}), bf16[8,512,256]{2,1,0:T(8,128)(2,1)}, u32[]{:S(2)}, u32[]{:S(2)}) %all-to-all-start.1) | async-done | bytes 2097184 | tf_op jit(solution)/shard_map/all_to_all | solution.py:155
  972.8 51.9 %reduce-scatter.2.cloned.1.call-done = f32[1,64,512]{2,1,0:T(8,128)} async-done(((f32[32,64,512]{2,1,0:T(8,128)}), f32[1,64,512]{2,1,0:T(8,128)}) %reduce-scatter.2.cloned.1.call-update) | async-done | bytes 131088 | tf_op jit(solution)/shard_map/reduce_scatter | solution.py:183
  (127 shorter events, 45.2 us)
Async XLA Ops:
  7.2 145.8 %copy-start = (bf16[512,2048]{1,0:T(8,128)(2,1)S(1)}, bf16[512,2048]{1,0:T(8,128)(2,1)}, u32[]{:S(2)}) copy-start(bf16[512,2048]{1,0:T(8,128)(2,1)} %param.31) | copy-start | bytes 6291460
  7.2 25.2 %copy-start.2 = (s32[64,32]{0,1:T(8,128)S(1)}, s32[64,32]{0,1:T(8,128)}, u32[]{:S(2)}) copy-start(s32[64,32]{0,1:T(8,128)} %param.35) | copy-start | bytes 24580
  7.2 25.3 %copy-start.16 = (f32[128]{0:T(128)S(1)}, f32[128]{0:T(128)}, u32[]{:S(2)}) copy-start(f32[128]{0:T(128)} %param.25) | copy-start | bytes 1540
  7.2 829.2 %all-reduce.3.cloned.1.call-start = ((), (), s32[]{:S(2)}) async-start(), calls=%async_computation.3 | async-start | bytes 1048576 | tf_op jit(solution)/shard_map/psum | solution.py:164
  28.7 0.7 copy-start.4
  32.8 4.6 copy-start.8
  32.8 4.6 copy-start.10
  37.4 46.3 %copy-start.6 = (pred[64,4096]{1,0:T(8,128)(4,1)S(1)}, pred[64,4096]{1,0:T(8,128)(4,1)}, u32[]{:S(2)}) copy-start(pred[64,4096]{1,0:T(8,128)(4,1)} %iota_compare_fusion) | copy-start | bytes 786436
  83.7 5.3 copy-start.5
  83.7 5.3 copy-start.12
  83.7 5.3 copy-start.15
  83.7 7.1 copy-start.17
  83.7 7.2 copy-start.9
  83.7 7.2 copy-start.11
  152.9 684.7 %copy-start.13 = (f32[2048]{0:T(1024)S(1)}, f32[2048]{0:T(1024)}, u32[]{:S(2)}) copy-start(f32[2048]{0:T(1024)} %param.38) | copy-start | bytes 24580
  156.3 710.5 %all-gather.2.cloned.1.call-start = ((), (), s32[]{:S(2)}) async-start(), calls=%async_computation.4 | async-start | bytes 2359296 | tf_op jit(solution)/shard_map/all_gather | solution.py:171
  838.5 186.1 %reduce-scatter.2.cloned.1.call-start = ((), (), s32[]{:S(2)}) async-start(), calls=%async_computation.5 | async-start | bytes 4325376 | tf_op jit(solution)/shard_map/reduce_scatter | solution.py:183
  866.8 2.8 copy-start.19
  869.6 3.8 copy-start.7
  876.1 0.8 copy-start.3
  885.5 6.4 copy-start.1
  885.5 7.8 copy-start.21
  902.9 34.9 %all-to-all-start = ((bf16[8,512,256]{2,1,0:T(8,128)(2,1)}), bf16[8,512,256]{2,1,0:T(8,128)(2,1)}, u32[]{:S(2)}, u32[]{:S(2)}) async-start(bf16[8,512,256]{2,1,0:T(8,128)(2,1)} %gather_fusion.5), calls=%async_computation.1 | async-start | bytes 4194304 | tf_op jit(solution)/shard_map/all_to_all | solution.py:152
  937.8 35.0 %all-to-all-start.1 = ((bf16[8,512,256]{2,1,0:T(8,128)(2,1)}), bf16[8,512,256]{2,1,0:T(8,128)(2,1)}, u32[]{:S(2)}, u32[]{:S(2)}) async-start(bf16[8,512,256]{2,1,0:T(8,128)(2,1)} %gather_fusion.8), calls=%async_computation.2 | async-start | bytes 4194304 | tf_op jit(solution)/shard_map/all_to_all | solution.py:155
  (3 other events, 1.9 us)
Sparse Core Ops, SparseCore 0:
  156.5 679.9 all-reduce.2
  838.9 27.8 all-gather.1
  876.2 148.3 reduce-scatter.1
where the time goes:
time: 1050 us; the launch traced here: 1040 us
  waiting for transfers between devices  818 us (78%)
  local copies, waits for them, and re-layouts  113 us (11%)
  matrix products  34.2 us (3%)
  other arithmetic  32.3 us (3%)
  between operations  16.9 us (2%)
  blocking collectives  15.8 us (2%)
    psum x1, waiting for transfers between devices, per_device(): attn_sum = lax.psum(head_terms, 'kv')  680 us
    reduce_scatter x1, waiting for transfers between devices, per_device(): lax.psum_scatter(term, ('req', 'kv'), scatter_dimension=0, tiled=True)[0]  51.9 us
    all_to_all x1, waiting for transfers between devices, per_device(): lax.all_to_all(place_cache(v_pool, new_values), 'req', split_axis=0, conc...  30.6 us
    all_gather x1, waiting for transfers between devices, per_device(): row_piece = lax.all_gather(normed_mlp, 'req', axis=0, tiled=True)  28.2 us
    all_to_all x1, waiting for transfers between devices, per_device(): lax.all_to_all(place_cache(k_pool, new_keys), 'req', split_axis=0, concat...  26.9 us
    reshape x1, local copies, waits for them, and re-layouts, value_block(): v_pool[page_ids].reshape(req_count, block_width, kv_local, head_dim)  23.7 us
    reshape x1, local copies, waits for them, and re-layouts, score_block(): k_pool[page_ids].reshape(req_count, block_width, kv_local, head_dim)  23.7 us
  transfers between devices with their start and end apart: 5, of which 5 were waited for; matrix products, arithmetic and copies ran while one was open for 3% of the time, Pallas kernels for 0%

commit v1 on v0

v1 whole, which is shorter than its diff:
```python
import functools

import jax
import jax.numpy as jnp
from jax import lax
from jax.experimental import pallas as pl
from jax.experimental.pallas import tpu as pltpu
from jax.sharding import PartitionSpec as P

MIGP = 4
EPSILON = 1e-06
ROPE_BASE = 1000000.0
ROWS = 8
LOW = -1e30


def rms_norm(values, scale_row):
    values = values.astype(jnp.float32)
    return (
        values * lax.rsqrt(jnp.mean(values * values, axis=-1, keepdims=True) + EPSILON) * scale_row
    )


def rotate(values, position):
    half_dim = values.shape[-1] // 2
    frequency = ROPE_BASE ** (-jnp.arange(half_dim, dtype=jnp.float32) * 2.0 / values.shape[-1])
    angles = position.astype(jnp.float32)[:, None, None] * frequency
    cosine = jnp.cos(angles)
    sine_part = jnp.sin(angles)
    first_half = values[..., :half_dim]
    second = values[..., half_dim:]
    return jnp.concatenate(
        [first_half * cosine - second * sine_part, second * cosine + first_half * sine_part],
        axis=-1,
    )


def page_owners(page_table, lengths, pool_pages, page_size):
    req_count, slots = page_table.shape
    slot = jnp.arange(slots, dtype=jnp.int32)[None, :]
    used = slot <= (lengths // page_size)[:, None]
    table = jnp.where(used, page_table, -1).reshape(1, -1)
    code = jnp.arange(req_count * slots, dtype=jnp.int32)[None, :]
    hit = table == jnp.arange(pool_pages, dtype=jnp.int32)[:, None]
    return jnp.max(jnp.where(hit, code, -1), axis=1)


def attend_kernel(
    slots, group, blocks, per_block, page_size, scale,
    code_ref, len_ref, q_ref, k_new_ref, v_new_ref, k_ref, v_ref,
    out_ref, scores, top, total, acc,
):
    step = pl.program_id(0)
    head_dim = out_ref.shape[-1]
    kv_local = k_ref.shape[-1] // head_dim
    lane = lax.broadcasted_iota(jnp.int32, (ROWS, page_size), 1)
    row = lax.broadcasted_iota(jnp.int32, (ROWS, head_dim), 0)

    def own_scores():
        folded = q_ref[:, :, :head_dim]
        for k in range(1, kv_local):
            folded = folded + q_ref[:, :, k * head_dim : (k + 1) * head_dim]
        return jnp.sum(folded * k_new_ref[...], axis=-1, keepdims=True) * scale

    @pl.when(step == 0)
    def _():
        top[...] = jnp.broadcast_to(own_scores(), top.shape)

    @pl.when(step < blocks)
    def _():
        for j in range(per_block):
            page = step * per_block + j
            code = code_ref[page]
            owner = jnp.maximum(code, 0) // slots
            left = jnp.where(code < 0, 0, len_ref[owner] - lax.rem(code, slots) * page_size)
            s = lax.dot_general(
                q_ref[owner].astype(jnp.bfloat16),
                k_ref[j],
                (((1,), (1,)), ((), ())),
                preferred_element_type=jnp.float32,
            )
            s = jnp.where(lane < left, s * scale, LOW)
            scores[page] = s
            top[owner] = jnp.maximum(top[owner], s)

    @pl.when(step == blocks)
    def _():
        peak = jnp.max(top[...], axis=-1, keepdims=True)
        top[...] = jnp.broadcast_to(peak, top.shape)
        own = jnp.exp(own_scores() - peak)
        wide_lane = lax.broadcasted_iota(jnp.int32, total.shape, 2)
        total[...] = jnp.where(wide_lane == 0, own, 0.0)
        acc[...] = own * v_new_ref[...]

    @pl.when(step >= blocks)
    def _():
        for j in range(per_block):
            page = (step - blocks) * per_block + j
            owner = jnp.maximum(code_ref[page], 0) // slots
            e = jnp.exp(scores[page] - top[owner])
            total[owner] = total[owner] + e
            o = jnp.dot(e.astype(jnp.bfloat16), v_ref[j], preferred_element_type=jnp.float32)
            picked = o[:, :head_dim]
            for k in range(1, kv_local):
                picked = jnp.where(
                    row // group == k, o[:, k * head_dim : (k + 1) * head_dim], picked
                )
            acc[owner] = acc[owner] + picked

    @pl.when(step == 2 * blocks - 1)
    def _():
        out_ref[...] = acc[...] / jnp.sum(total[...], axis=-1, keepdims=True)


def attend(queries, new_keys, new_values, k_pool, v_pool, lengths, page_table):
    req_count, kv_local, group, head_dim = queries.shape
    pool_pages, page_size, channels = k_pool.shape
    slots = page_table.shape[1]
    heads = kv_local * group
    per_block = max(b for b in range(1, 17) if pool_pages % b == 0)
    blocks = pool_pages // per_block
    code = page_owners(page_table, lengths, pool_pages, page_size)
    which = jnp.eye(kv_local, dtype=jnp.float32)[None, :, None, :, None]
    spread = (queries.astype(jnp.float32)[:, :, :, None, :] * which).reshape(
        req_count, heads, channels
    )
    pad = ((0, 0), (0, ROWS - heads), (0, 0))
    spread = jnp.pad(spread, pad)

    def by_head(values):
        values = jnp.repeat(values.astype(jnp.float32), group, axis=1)
        return jnp.pad(values, pad)

    whole = pl.BlockSpec((req_count, ROWS, channels), lambda i, *_: (0, 0, 0))
    slim = pl.BlockSpec((req_count, ROWS, head_dim), lambda i, *_: (0, 0, 0))
    out = pl.pallas_call(
        functools.partial(
            attend_kernel, slots, group, blocks, per_block, page_size, head_dim ** (-0.5)
        ),
        out_shape=jax.ShapeDtypeStruct((req_count, ROWS, head_dim), jnp.float32),
        grid_spec=pltpu.PrefetchScalarGridSpec(
            num_scalar_prefetch=2,
            grid=(2 * blocks,),
            in_specs=[
                whole,
                slim,
                slim,
                pl.BlockSpec(
                    (per_block, page_size, channels),
                    lambda i, *_: (jnp.minimum(i, blocks - 1), 0, 0),
                ),
                pl.BlockSpec(
                    (per_block, page_size, channels),
                    lambda i, *_: (jnp.maximum(i - blocks, 0), 0, 0),
                ),
            ],
            out_specs=slim,
            scratch_shapes=[
                pltpu.VMEM((pool_pages, ROWS, page_size), jnp.float32),
                pltpu.VMEM((req_count, ROWS, page_size), jnp.float32),
                pltpu.VMEM((req_count, ROWS, page_size), jnp.float32),
                pltpu.VMEM((req_count, ROWS, head_dim), jnp.float32),
            ],
        ),
        compiler_params=pltpu.CompilerParams(
            dimension_semantics=("arbitrary",), vmem_limit_bytes=32 * 1024 * 1024
        ),
        cost_estimate=pl.CostEstimate(
            flops=4 * pool_pages * page_size * channels * ROWS,
            bytes_accessed=2 * pool_pages * page_size * channels * 2,
            transcendentals=pool_pages * page_size * ROWS,
        ),
        name="attend_pool",
    )(code, lengths, spread, by_head(new_keys), by_head(new_values), k_pool, v_pool)
    return out[:, :heads]


def pack_kernel(page_ref, len_ref, *refs):
    pages = MIGP
    out_ref = refs[2 * pages]
    page_size = refs[0].shape[1]
    row = lax.broadcasted_iota(jnp.int32, refs[0].shape[1:], 0)
    for side in range(2):
        for t in range(pages):
            block = refs[side * pages + t][0]
            keep = row + t * page_size < len_ref[0]
            out_ref[side, t * page_size : (t + 1) * page_size] = jnp.where(
                keep, block, jnp.zeros_like(block)
            )


def pack_block(pages, length, k_pool, v_pool):
    _, page_size, channels = k_pool.shape
    span = MIGP * page_size

    def page_spec(t):
        return pl.BlockSpec((1, page_size, channels), lambda i, page_ref, len_ref: (page_ref[t], 0, 0))

    return pl.pallas_call(
        pack_kernel,
        out_shape=jax.ShapeDtypeStruct((2, span, channels), jnp.bfloat16),
        grid_spec=pltpu.PrefetchScalarGridSpec(
            num_scalar_prefetch=2,
            grid=(1,),
            in_specs=[page_spec(t) for _ in range(2) for t in range(MIGP)],
            out_specs=pl.BlockSpec((2, span, channels), lambda i, *_: (0, 0, 0)),
        ),
        cost_estimate=pl.CostEstimate(
            flops=0, bytes_accessed=8 * span * channels, transcendentals=0
        ),
        name="pack_block",
    )(pages, length, *([k_pool] * MIGP), *([v_pool] * MIGP))


def place_kernel(count, where_ref, len_ref, fresh_ref, *refs):
    blocks, k_out, v_out = refs[:count], refs[count], refs[count + 1]
    span, channels = blocks[0].shape[1:]
    row = lax.broadcasted_iota(jnp.int32, (span, channels), 0)
    for s in range(count):
        slot = where_ref[s]
        for side, out in enumerate((k_out, v_out)):
            new = fresh_ref[s, :, side * channels : (side + 1) * channels]
            out[slot] = jnp.where(row == len_ref[s], new, blocks[s][side])


def place_blocks(where, lengths, fresh, blocks):
    count = len(blocks)
    _, span, channels = blocks[0].shape
    shape = jax.ShapeDtypeStruct((count, span, channels), jnp.bfloat16)
    smem = pl.BlockSpec(memory_space=pltpu.SMEM)
    vmem = pl.BlockSpec(memory_space=pltpu.VMEM)
    return pl.pallas_call(
        functools.partial(place_kernel, count),
        out_shape=(shape, shape),
        in_specs=[smem, smem, vmem] + [vmem] * count,
        out_specs=(vmem, vmem),
        compiler_params=pltpu.CompilerParams(vmem_limit_bytes=40 * 1024 * 1024),
        name="place_blocks",
    )(where, lengths, fresh, *blocks)


def per_device(
    hidden,
    attn_gain,
    q_gain,
    k_gain,
    w_q,
    w_gate_attn,
    w_k,
    w_v,
    w_o,
    k_pool,
    v_pool,
    lengths,
    page_table,
    mig_request,
    mig_dest,
    mlp_gain,
    w_gate,
    w_up,
    w_down,
):
    head_dim = q_gain.shape[0]
    req_count = hidden.shape[0]
    kv_local = w_k.shape[1] // head_dim
    q_local = w_q.shape[1] // head_dim
    group_size = q_local // kv_local
    channels = kv_local * head_dim
    model_width = mlp_gain.shape[0]
    req_groups = lax.axis_size("req")
    me = lax.axis_index("req")

    mig_rows = mig_request[0]
    dest_row = mig_dest[0]
    partner = me ^ jnp.arange(req_groups, dtype=jnp.int32)
    chosen = dest_row[None, :] == partner[:, None]
    send_rows = jnp.sum(jnp.where(chosen, mig_rows[None, :], 0), axis=1)
    send_len = lengths[send_rows]
    send_pages = page_table[send_rows, :MIGP]
    packed = [
        pack_block(send_pages[s], send_len[s : s + 1], k_pool, v_pool) for s in range(req_groups)
    ]
    arrived = [packed[0]] + [
        lax.ppermute(packed[s], "req", [(i, i ^ s) for i in range(req_groups)])
        for s in range(1, req_groups)
    ]

    whole_rows = lax.all_gather(hidden, "kv", axis=1, tiled=True)
    normed = rms_norm(whole_rows, attn_gain).astype(jnp.bfloat16)
    query_raw = jnp.dot(normed, w_q, preferred_element_type=jnp.float32).reshape(
        req_count, q_local, head_dim
    )
    gate_raw = jnp.dot(normed, w_gate_attn, preferred_element_type=jnp.float32)
    key_raw = jnp.dot(normed, w_k, preferred_element_type=jnp.float32).reshape(
        req_count, kv_local, head_dim
    )
    value_raw = jnp.dot(normed, w_v, preferred_element_type=jnp.float32).reshape(
        req_count, kv_local, head_dim
    )
    queries = rotate(rms_norm(query_raw, q_gain), lengths).astype(jnp.bfloat16)
    queries = queries.reshape(req_count, kv_local, group_size, head_dim)
    new_keys = rotate(rms_norm(key_raw, k_gain), lengths).astype(jnp.bfloat16)
    new_values = value_raw.astype(jnp.bfloat16)

    fresh = jnp.concatenate(
        [new_keys.reshape(req_count, channels), new_values.reshape(req_count, channels)], axis=1
    )
    by_dest = jnp.sum(
        jnp.where(
            dest_row[None, :] == jnp.arange(req_groups, dtype=jnp.int32)[:, None],
            mig_rows[None, :],
            0,
        ),
        axis=1,
    )
    dest_len = lengths[by_dest]
    digits = jnp.stack([dest_len // 256, dest_len % 256], axis=1).astype(jnp.bfloat16)
    notes = jnp.concatenate([fresh[by_dest], jnp.pad(digits, ((0, 0), (0, 126)))], axis=1)
    all_notes = lax.all_gather(notes, "req", axis=0, tiled=False)
    mine = lax.dynamic_index_in_dim(all_notes, me, 1, keepdims=False)[partner]
    width = 2 * channels
    got_digits = mine[:, width : width + 2].astype(jnp.int32)
    got_len = got_digits[:, 0] * 256 + got_digits[:, 1]
    mig_keys, mig_values = place_blocks(partner, got_len, mine[:, None, :width], arrived)

    context = attend(queries, new_keys, new_values, k_pool, v_pool, lengths, page_table)
    gated = (jax.nn.sigmoid(gate_raw) * context.reshape(req_count, q_local * head_dim)).astype(
        jnp.bfloat16
    )
    head_terms = jnp.dot(gated, w_o, preferred_element_type=jnp.float32)
    attn_sum = lax.psum(head_terms, "kv")
    mid_stream = (whole_rows.astype(jnp.float32) + attn_sum).astype(jnp.bfloat16)
    normed_mlp = rms_norm(mid_stream, mlp_gain).astype(jnp.bfloat16)
    kv_count = lax.axis_size("kv")
    slice_width = model_width // kv_count
    slice_start = lax.axis_index("kv") * slice_width
    mid_slice = lax.dynamic_slice_in_dim(mid_stream, slice_start, slice_width, 1)
    row_piece = lax.all_gather(normed_mlp, "req", axis=0, tiled=True)
    gate_part = jnp.dot(row_piece, w_gate, preferred_element_type=jnp.float32)
    up_part = jnp.dot(row_piece, w_up, preferred_element_type=jnp.float32)
    activation = (jax.nn.silu(gate_part) * up_part).astype(jnp.bfloat16)
    unit_count = activation.shape[1]
    grouped_act = activation.reshape(req_groups, req_count, unit_count)
    grouped_down = w_down.reshape(kv_count, slice_width, unit_count)
    term = jnp.einsum(
        "gru,hcu->ghrc", grouped_act, grouped_down, preferred_element_type=jnp.float32
    )
    term = term.reshape(req_groups * kv_count, req_count, slice_width)
    mlp_part = lax.psum_scatter(term, ("req", "kv"), scatter_dimension=0, tiled=True)[0]
    out_hidden = (mid_slice.astype(jnp.float32) + mlp_part).astype(jnp.bfloat16)
    return (out_hidden, mig_keys, mig_values)


def solution(mesh):
    return jax.shard_map(
        per_device,
        mesh=mesh,
        in_specs=(
            P("req", "kv"),
            P(),
            P(),
            P(),
            P(None, "kv"),
            P(None, "kv"),
            P(None, "kv"),
            P(None, "kv"),
            P("kv", None),
            P("req", None, "kv"),
            P("req", None, "kv"),
            P("req"),
            P("req", None),
            P("req", None),
            P("req", None),
            P(),
            P(None, ("req", "kv")),
            P(None, ("req", "kv")),
            P(None, ("req", "kv")),
        ),
        out_specs=(P("req", "kv"), P("req", None, "kv"), P("req", None, "kv")),
        check_vma=False,
    )
```

time: 1050 us -> 297 us (0.28)
  waiting for transfers between devices: 818 us -> 143 us
  local copies, waits for them, and re-layouts: 113 us -> 23.3 us
  Pallas kernels: 0 us -> 38 us
  blocking collectives: 15.8 us -> 43 us
  other arithmetic: 32.3 us -> 12.9 us
  matrix products: 34.2 us -> 15 us
    psum x1, waiting for transfers between devices: 680 us -> 39.9 us  [per_device(): attn_sum = lax.psum(head_terms, 'kv')]
    all_to_all x2 -> x0, waiting for transfers between devices: 57.6 us -> none  [the longest x1 30.6 us: per_device(): lax.all_to_all(place_cache(v_pool, new_values), 'req', split_axis=0, conc...]
    reshape x3 -> x0, local copies, waits for them, and re-layouts: 47.5 us -> none  [the longest x1 23.7 us: value_block(): v_pool[page_ids].reshape(req_count, block_width, kv_local, head_dim)]
    gather x13 -> x9, local copies, waits for them, and re-layouts: 50.5 us -> 5.11 us  [the longest x4 2.58 us: per_device(): send_pages = page_table[send_rows, :MIGP]]
    pallas_call x0 -> x10, Pallas kernels: none -> 38 us  [the longest x8 25.8 us: pack_block(): pl.pallas_call(pack_kernel, out_shape=jax.ShapeDtypeStruct((2, span, chan...]
    all_gather x0 -> x1, blocking collectives: none -> 27.2 us  [per_device(): all_notes = lax.all_gather(notes, 'req', axis=0, tiled=False)]
    ppermute x0 -> x7, waiting for transfers between devices: none -> 24.1 us  [per_device(): lax.ppermute(packed[s], 'req', [(i, i ^ s) for i in range(req_groups)])]
    dot_general x3 -> x0, matrix products: 17.4 us -> none  [the longest x1 8.81 us: score_block(): jnp.einsum('rkgd,rtkd->rkgt', queries, key_block, preferred_element_type=...]
  transfers between devices with their start and end apart: 5 -> 10, of which waited for: 5 -> 5; matrix products, arithmetic and copies ran while one was open for 3% -> 3% of each run, Pallas kernels for 0% -> 10%
where the time goes in v1:
time: 297 us; the launch traced here: 296 us
  waiting for transfers between devices  143 us (48%)
  blocking collectives  43 us (14%)
  Pallas kernels  38 us (13%)
  local copies, waits for them, and re-layouts  23.3 us (8%)
  matrix products  15 us (5%)
  between operations  14.2 us (5%)
  other arithmetic  12.9 us (4%)
  starting transfers between devices  6.47 us (2%)
    reduce_scatter x1, waiting for transfers between devices, per_device(): lax.psum_scatter(term, ('req', 'kv'), scatter_dimension=0, tiled=True)[0]  50.7 us
    psum x1, waiting for transfers between devices, per_device(): attn_sum = lax.psum(head_terms, 'kv')  39.9 us
    all_gather x1, waiting for transfers between devices, per_device(): row_piece = lax.all_gather(normed_mlp, 'req', axis=0, tiled=True)  28 us
    all_gather x1, blocking collectives, per_device(): all_notes = lax.all_gather(notes, 'req', axis=0, tiled=False)  27.2 us
    pallas_call x8, Pallas kernels, pack_block(): pl.pallas_call(pack_kernel, out_shape=jax.ShapeDtypeStruct((2, span, chan...  25.8 us
    ppermute x7, waiting for transfers between devices, per_device(): lax.ppermute(packed[s], 'req', [(i, i ^ s) for i in range(req_groups)])  24.1 us
    all_gather x1, blocking collectives, per_device(): whole_rows = lax.all_gather(hidden, 'kv', axis=1, tiled=True)  15.8 us
    unnamed x44, local copies, waits for them, and re-layouts  11.3 us
  transfers between devices with their start and end apart: 10, of which 5 were waited for; matrix products, arithmetic and copies ran while one was open for 3% of the time, Pallas kernels for 10%

profile of v1, /device:TPU:0, one launch (start us, length us, event | category | flops | bytes accessed | tf_op | source)
XLA Modules:
  0.0 295.6 jit_solution(2133490517750071410)
XLA Ops:
  10.8 15.8 %all_gather.12 = bf16[64,2048]{1,0:T(8,128)(2,1)S(1)} all-gather(bf16[64,512]{1,0:T(8,128)(2,1)} %param.19), channel_id=1, replica_groups=mesh['req'=8,'kv'=4] {'kv'}, dimensions={1}, use_global_device_ids=true | all-gather | bytes 327680 | tf_op jit(solution)/shard_map/all_gather | solution.py:288
  26.8 2.9 fusion.32
  41.6 3.8 %copy-done.1 = bf16[150,128,256]{2,1,0:T(8,128)(2,1)S(1)} copy-done((bf16[150,128,256]{2,1,0:T(8,128)(2,1)S(1)}, bf16[150,128,256]{2,1,0:T(8,128)(2,1)}, u32[]{:S(2)}) %copy-start.1) | copy-done | bytes 9830424
  45.4 3.8 %copy-done.2 = bf16[150,128,256]{2,1,0:T(8,128)(2,1)S(1)} copy-done((bf16[150,128,256]{2,1,0:T(8,128)(2,1)S(1)}, bf16[150,128,256]{2,1,0:T(8,128)(2,1)}, u32[]{:S(2)}) %copy-start.2) | copy-done | bytes 9830424
  49.1 7.9 %attend_pool.1 = f32[64,8,128]{2,1,0:T(8,128)S(1)} custom-call(s32[150]{0:T(256)S(1)} %select_reduce_fusion.code_ref, s32[64]{0:T(128)S(1)} %copy-done.3, f32[64,8,256]{2,1,0:T(8,128)S(1)} %pad.16.q_ref, f32[64,8,128]{2,1,0:T(8,128)S(1)} %pad.17.k_new_ref, f32[64,8,128]{2,1,0:T(8,128)S(1)} %pad.18.v_new_ref, bf16[150,128,256]{2,1,0:T(8,128)(2,1)S(1)} %copy-done.1, ...), custom_call_target="tpu_custom_call" | custom-call | flops 157286400 | bytes 19660800 | tf_op jit(solution)/shard_map/attend_pool/pallas_call | solution.py:136
  57.1 3.4 %fusion.6 = f32[64,2048]{1,0:T(8,128)} fusion(bf16[512,2048]{1,0:T(8,128)(2,1)S(1)} %copy-done, bf16[2048,512]{1,0:T(8,128)(2,1)} %param.24, f32[8,8,4,128]{3,2,1,0:T(4,128)S(1)} %bitcast.74, bf16[64,2048]{1,0:T(8,128)(2,1)S(1)} %all_gather.12, f32[2048]{0:T(1024)S(1)} %copy-done.12, f32[64]{0:T(128)S(1)} %copy-done.15), kind=kOutput, calls=%fused_computation.18 | convolution fusion | flops 269123584 | bytes 5120256 | tf_op jit(solution)/shard_map/dot_general | solution.py:330
  60.6 39.9 %all-reduce.7.cloned.1.call-done = f32[64,2048]{1,0:T(8,128)} async-done(((f32[64,2048]{1,0:T(8,128)}), f32[64,2048]{1,0:T(8,128)}) %all-reduce.7.cloned.1.call-update) | async-done | bytes 524304 | tf_op jit(solution)/shard_map/psum | solution.py:331
  103.4 28.0 %all-gather.3.cloned.1.call-done = bf16[512,2048]{1,0:T(8,128)(2,1)} async-done(((bf16[64,2048]{1,0:T(8,128)(2,1)}), bf16[512,2048]{1,0:T(8,128)(2,1)}) %all-gather.3.cloned.1.call-update) | async-done | bytes 2097168 | tf_op jit(solution)/shard_map/all_gather | solution.py:338
  131.4 2.8 fusion.39
  134.1 2.1 fusion
  136.4 2.6 fusion.7
  145.3 3.3 %pack_block.9 = bf16[2,512,256]{2,1,0:T(8,128)(2,1)} custom-call(s32[4]{0:T(128)} %get-tuple-element.13.page_ref, s32[1]{0:T(128)} %get-tuple-element.39.len_ref, bf16[150,128,256]{2,1,0:T(8,128)(2,1)} %refs_3_.15, bf16[150,128,256]{2,1,0:T(8,128)(2,1)} %refs_3_.15, bf16[150,128,256]{2,1,0:T(8,128)(2,1)} %refs_3_.15, bf16[150,128,256]{2,1,0:T(8,128)(2,1)} %refs_3_.15, ...), custom_call_target="tpu_custom_call" | custom-call | bytes 1048576 | tf_op jit(solution)/shard_map/pack_block/pallas_call | solution.py:199
  148.9 3.2 %pack_block.10 = bf16[2,512,256]{2,1,0:T(8,128)(2,1)} custom-call(s32[4]{0:T(128)} %get-tuple-element.12.page_ref, s32[1]{0:T(128)} %get-tuple-element.38.len_ref, bf16[150,128,256]{2,1,0:T(8,128)(2,1)} %refs_3_.15, bf16[150,128,256]{2,1,0:T(8,128)(2,1)} %refs_3_.15, bf16[150,128,256]{2,1,0:T(8,128)(2,1)} %refs_3_.15, bf16[150,128,256]{2,1,0:T(8,128)(2,1)} %refs_3_.15, ...), custom_call_target="tpu_custom_call" | custom-call | bytes 1048576 | tf_op jit(solution)/shard_map/pack_block/pallas_call | solution.py:199
  153.6 3.2 %pack_block.11 = bf16[2,512,256]{2,1,0:T(8,128)(2,1)} custom-call(s32[4]{0:T(128)} %get-tuple-element.11.page_ref, s32[1]{0:T(128)} %get-tuple-element.37.len_ref, bf16[150,128,256]{2,1,0:T(8,128)(2,1)} %refs_3_.15, bf16[150,128,256]{2,1,0:T(8,128)(2,1)} %refs_3_.15, bf16[150,128,256]{2,1,0:T(8,128)(2,1)} %refs_3_.15, bf16[150,128,256]{2,1,0:T(8,128)(2,1)} %refs_3_.15, ...), custom_call_target="tpu_custom_call" | custom-call | bytes 1048576 | tf_op jit(solution)/shard_map/pack_block/pallas_call | solution.py:199
  156.9 3.2 %pack_block.12 = bf16[2,512,256]{2,1,0:T(8,128)(2,1)} custom-call(s32[4]{0:T(128)} %get-tuple-element.10.page_ref, s32[1]{0:T(128)} %get-tuple-element.36.len_ref, bf16[150,128,256]{2,1,0:T(8,128)(2,1)} %refs_3_.15, bf16[150,128,256]{2,1,0:T(8,128)(2,1)} %refs_3_.15, bf16[150,128,256]{2,1,0:T(8,128)(2,1)} %refs_3_.15, bf16[150,128,256]{2,1,0:T(8,128)(2,1)} %refs_3_.15, ...), custom_call_target="tpu_custom_call" | custom-call | bytes 1048576 | tf_op jit(solution)/shard_map/pack_block/pallas_call | solution.py:199
  161.5 3.2 %pack_block.13 = bf16[2,512,256]{2,1,0:T(8,128)(2,1)} custom-call(s32[4]{0:T(128)} %get-tuple-element.9.page_ref, s32[1]{0:T(128)} %get-tuple-element.35.len_ref, bf16[150,128,256]{2,1,0:T(8,128)(2,1)} %refs_3_.15, bf16[150,128,256]{2,1,0:T(8,128)(2,1)} %refs_3_.15, bf16[150,128,256]{2,1,0:T(8,128)(2,1)} %refs_3_.15, bf16[150,128,256]{2,1,0:T(8,128)(2,1)} %refs_3_.15, ...), custom_call_target="tpu_custom_call" | custom-call | bytes 1048576 | tf_op jit(solution)/shard_map/pack_block/pallas_call | solution.py:199
  167.1 27.2 %all-gather = bf16[64,640]{1,0:T(8,128)(2,1)S(1)} all-gather(bf16[8,640]{1,0:T(8,128)(2,1)S(1)} %fusion.22), channel_id=2, replica_groups=mesh['req'=8,'kv'=4] {'req'}, dimensions={0}, use_global_device_ids=true | all-gather | bytes 92160 | tf_op jit(solution)/shard_map/all_gather | solution.py:319
  195.0 3.2 %pack_block.14 = bf16[2,512,256]{2,1,0:T(8,128)(2,1)} custom-call(s32[4]{0:T(128)} %get-tuple-element.8.page_ref, s32[1]{0:T(128)} %get-tuple-element.34.len_ref, bf16[150,128,256]{2,1,0:T(8,128)(2,1)} %refs_3_.15, bf16[150,128,256]{2,1,0:T(8,128)(2,1)} %refs_3_.15, bf16[150,128,256]{2,1,0:T(8,128)(2,1)} %refs_3_.15, bf16[150,128,256]{2,1,0:T(8,128)(2,1)} %refs_3_.15, ...), custom_call_target="tpu_custom_call" | custom-call | bytes 1048576 | tf_op jit(solution)/shard_map/pack_block/pallas_call | solution.py:199
  198.2 3.3 %pack_block.15 = bf16[2,512,256]{2,1,0:T(8,128)(2,1)} custom-call(s32[4]{0:T(128)} %get-tuple-element.7.page_ref, s32[1]{0:T(128)} %get-tuple-element.33.len_ref, bf16[150,128,256]{2,1,0:T(8,128)(2,1)} %refs_3_.15, bf16[150,128,256]{2,1,0:T(8,128)(2,1)} %refs_3_.15, bf16[150,128,256]{2,1,0:T(8,128)(2,1)} %refs_3_.15, bf16[150,128,256]{2,1,0:T(8,128)(2,1)} %refs_3_.15, ...), custom_call_target="tpu_custom_call" | custom-call | bytes 1048576 | tf_op jit(solution)/shard_map/pack_block/pallas_call | solution.py:199
  204.1 3.2 %pack_block.8.refs_0_ = bf16[2,512,256]{2,1,0:T(8,128)(2,1)} custom-call(s32[4]{0:T(128)} %get-tuple-element.14.page_ref, s32[1]{0:T(128)} %get-tuple-element.40.len_ref, bf16[150,128,256]{2,1,0:T(8,128)(2,1)} %refs_3_.15, bf16[150,128,256]{2,1,0:T(8,128)(2,1)} %refs_3_.15, bf16[150,128,256]{2,1,0:T(8,128)(2,1)} %refs_3_.15, ...), custom_call_target="tpu_custom_call" | custom-call | bytes 1048576 | tf_op jit(solution)/shard_map/pack_block/pallas_call | solution.py:199
  207.5 12.1 %collective-permute-done.5.refs_6_ = bf16[2,512,256]{2,1,0:T(8,128)(2,1)} collective-permute-done((bf16[2,512,256]{2,1,0:T(8,128)(2,1)}, bf16[2,512,256]{2,1,0:T(8,128)(2,1)}, u32[]{:S(2)}, u32[]{:S(2)}) %collective-permute-start.5) | collective-permute-done | bytes 524320 | tf_op jit(solution)/shard_map/ppermute | solution.py:284
  219.6 12.0 %collective-permute-done.6.refs_7_ = bf16[2,512,256]{2,1,0:T(8,128)(2,1)} collective-permute-done((bf16[2,512,256]{2,1,0:T(8,128)(2,1)}, bf16[2,512,256]{2,1,0:T(8,128)(2,1)}, u32[]{:S(2)}, u32[]{:S(2)}) %collective-permute-start.6) | collective-permute-done | bytes 524320 | tf_op jit(solution)/shard_map/ppermute | solution.py:284
  232.6 4.3 %place_blocks.1 = (bf16[8,512,256]{2,1,0:T(8,128)(2,1)}, bf16[8,512,256]{2,1,0:T(8,128)(2,1)}) custom-call(s32[8]{0:T(128)S(1)} %copy-done.6, s32[8]{0:T(128)S(1)} %add_reduce_fusion.len_ref, bf16[8,1,512]{2,1,0:T(2,128)(2,1)S(1)} %copy.126.fresh_ref, bf16[2,512,256]{2,1,0:T(8,128)(2,1)S(1)} %copy-done.4, ...), custom_call_target="tpu_custom_call" | custom-call | tf_op jit(solution)/shard_map/place_blocks/pallas_call | solution.py:232
  236.9 50.7 %reduce-scatter.2.cloned.1.call-done = f32[1,64,512]{2,1,0:T(8,128)} async-done(((f32[32,64,512]{2,1,0:T(8,128)}), f32[1,64,512]{2,1,0:T(8,128)}) %reduce-scatter.2.cloned.1.call-update) | async-done | bytes 131088 | tf_op jit(solution)/shard_map/reduce_scatter | solution.py:349
  (139 shorter events, 36.5 us)
Async XLA Ops:
  7.2 49.9 %copy-start = (bf16[512,2048]{1,0:T(8,128)(2,1)S(1)}, bf16[512,2048]{1,0:T(8,128)(2,1)}, u32[]{:S(2)}) copy-start(bf16[512,2048]{1,0:T(8,128)(2,1)} %param.27) | copy-start | bytes 6291460
  7.2 93.3 %all-reduce.7.cloned.1.call-start = ((), (), s32[]{:S(2)}) async-start(), calls=%async_computation.1 | async-start | bytes 1048576 | tf_op jit(solution)/shard_map/psum | solution.py:331
  26.8 6.9 %copy-start.14 = (f32[64]{0:T(128)}, f32[64]{0:T(128)S(1)}, u32[]{:S(2)}) copy-start(f32[64]{0:T(128)S(1)} %add_rsqrt_fusion.3) | copy-start | bytes 772
  26.8 10.1 %copy-start.9 = (bf16[2048,256]{1,0:T(8,128)(2,1)S(1)}, bf16[2048,256]{1,0:T(8,128)(2,1)}, u32[]{:S(2)}) copy-start(bf16[2048,256]{1,0:T(8,128)(2,1)} %param.25) | copy-start | bytes 3145732
  26.8 10.1 %copy-start.12 = (f32[2048]{0:T(1024)S(1)}, f32[2048]{0:T(1024)}, u32[]{:S(2)}) copy-start(f32[2048]{0:T(1024)} %param.20) | copy-start | bytes 24580
  37.8 3.2 %copy-start.15 = (f32[64]{0:T(128)S(1)}, f32[64]{0:T(128)}, u32[]{:S(2)}) copy-start(f32[64]{0:T(128)} %copy-done.14) | copy-start | bytes 772
  37.9 3.2 %copy-start.10 = (bf16[2048,256]{1,0:T(8,128)(2,1)S(1)}, bf16[2048,256]{1,0:T(8,128)(2,1)}, u32[]{:S(2)}) copy-start(bf16[2048,256]{1,0:T(8,128)(2,1)} %param.26) | copy-start | bytes 3145732
  39.0 2.6 copy-start.3
  41.6 3.8 %copy-start.1 = (bf16[150,128,256]{2,1,0:T(8,128)(2,1)S(1)}, bf16[150,128,256]{2,1,0:T(8,128)(2,1)}, u32[]{:S(2)}) copy-start(bf16[150,128,256]{2,1,0:T(8,128)(2,1)} %refs_3_.15) | copy-start | bytes 29491204
  45.4 3.8 %copy-start.2 = (bf16[150,128,256]{2,1,0:T(8,128)(2,1)S(1)}, bf16[150,128,256]{2,1,0:T(8,128)(2,1)}, u32[]{:S(2)}) copy-start(bf16[150,128,256]{2,1,0:T(8,128)(2,1)} %refs_7_.15) | copy-start | bytes 29491204
  57.1 45.3 %copy-start.13 = (f32[2048]{0:T(1024)S(1)}, f32[2048]{0:T(1024)}, u32[]{:S(2)}) copy-start(f32[2048]{0:T(1024)} %param.34) | copy-start | bytes 24580
  60.5 70.8 %all-gather.3.cloned.1.call-start = ((), (), s32[]{:S(2)}) async-start(), calls=%async_computation.2 | async-start | bytes 2359296 | tf_op jit(solution)/shard_map/all_gather | solution.py:338
  103.3 184.2 %reduce-scatter.2.cloned.1.call-start = ((), (), s32[]{:S(2)}) async-start(), calls=%async_computation.3 | async-start | bytes 4325376 | tf_op jit(solution)/shard_map/reduce_scatter | solution.py:349
  131.4 2.8 copy-start.19
  134.1 2.2 copy-start.11
  139.0 1.3 copy-start.7
  148.6 52.9 %collective-permute-start = (bf16[2,512,256]{2,1,0:T(8,128)(2,1)}, bf16[2,512,256]{2,1,0:T(8,128)(2,1)S(1)}, u32[]{:S(2)}, u32[]{:S(2)}) collective-permute-start(bf16[2,512,256]{2,1,0:T(8,128)(2,1)} %pack_block.9), channel_id=1, source_target_pairs={{0,4},{4,0},{8,12},{12,8},{16,20},{20,16},{24,28},{28,24},{1,5},{5... | collective-permute-start | bytes 1572872 | tf_op jit(solution)/shard_map/ppermute | solution.py:284
  152.0 50.9 %collective-permute-start.1 = (bf16[2,512,256]{2,1,0:T(8,128)(2,1)}, bf16[2,512,256]{2,1,0:T(8,128)(2,1)S(1)}, u32[]{:S(2)}, u32[]{:S(2)}) collective-permute-start(bf16[2,512,256]{2,1,0:T(8,128)(2,1)} %pack_block.10), channel_id=1, source_target_pairs={{0,8},{4,12},{8,0},{12,4},{16,24},{20,28},{24,16},{28,20},{1,9},{5... | collective-permute-start | bytes 1572872 | tf_op jit(solution)/shard_map/ppermute | solution.py:284
  156.8 50.7 %collective-permute-start.2 = (bf16[2,512,256]{2,1,0:T(8,128)(2,1)}, bf16[2,512,256]{2,1,0:T(8,128)(2,1)}, u32[]{:S(2)}, u32[]{:S(2)}) collective-permute-start(bf16[2,512,256]{2,1,0:T(8,128)(2,1)} %pack_block.11), channel_id=1, source_target_pairs={{0,12},{4,8},{8,4},{12,0},{16,28},{20,24},{24,20},{28,16},{1,13},{... | collective-permute-start | bytes 1572872 | tf_op jit(solution)/shard_map/ppermute | solution.py:284
  160.1 47.4 %collective-permute-start.3 = (bf16[2,512,256]{2,1,0:T(8,128)(2,1)}, bf16[2,512,256]{2,1,0:T(8,128)(2,1)}, u32[]{:S(2)}, u32[]{:S(2)}) collective-permute-start(bf16[2,512,256]{2,1,0:T(8,128)(2,1)} %pack_block.12), channel_id=1, source_target_pairs={{0,16},{4,20},{8,24},{12,28},{16,0},{20,4},{24,8},{28,12},{1,17},{... | collective-permute-start | bytes 1572872 | tf_op jit(solution)/shard_map/ppermute | solution.py:284
  164.7 42.8 %collective-permute-start.4 = (bf16[2,512,256]{2,1,0:T(8,128)(2,1)}, bf16[2,512,256]{2,1,0:T(8,128)(2,1)}, u32[]{:S(2)}, u32[]{:S(2)}) collective-permute-start(bf16[2,512,256]{2,1,0:T(8,128)(2,1)} %pack_block.13), channel_id=1, source_target_pairs={{0,20},{4,16},{8,28},{12,24},{16,4},{20,0},{24,12},{28,8},{1,21},{... | collective-permute-start | bytes 1572872 | tf_op jit(solution)/shard_map/ppermute | solution.py:284
  201.5 18.1 %collective-permute-start.5 = (bf16[2,512,256]{2,1,0:T(8,128)(2,1)}, bf16[2,512,256]{2,1,0:T(8,128)(2,1)}, u32[]{:S(2)}, u32[]{:S(2)}) collective-permute-start(bf16[2,512,256]{2,1,0:T(8,128)(2,1)} %pack_block.14), channel_id=1, source_target_pairs={{0,24},{4,28},{8,16},{12,20},{16,8},{20,12},{24,0},{28,4},{1,25},{... | collective-permute-start | bytes 1572872 | tf_op jit(solution)/shard_map/ppermute | solution.py:284
  203.0 28.6 %collective-permute-start.6 = (bf16[2,512,256]{2,1,0:T(8,128)(2,1)}, bf16[2,512,256]{2,1,0:T(8,128)(2,1)}, u32[]{:S(2)}, u32[]{:S(2)}) collective-permute-start(bf16[2,512,256]{2,1,0:T(8,128)(2,1)} %pack_block.15), channel_id=1, source_target_pairs={{0,28},{4,24},{8,20},{12,16},{16,12},{20,8},{24,4},{28,0},{1,29},{... | collective-permute-start | bytes 1572872 | tf_op jit(solution)/shard_map/ppermute | solution.py:284
  204.1 27.5 %copy-start.6 = (s32[8]{0:T(128)S(1)}, s32[8]{0:T(128)}, u32[]{:S(2)}) copy-start(s32[8]{0:T(128)} %copy-done.5) | copy-start | bytes 100
  (6 other events, 4.6 us)
Sparse Core Ops, SparseCore 0:
  60.6 39.8 all-reduce.6
  103.4 27.8 all-gather.2
  139.2 148.3 reduce-scatter.1

commit v2 on v1

--- a/solution.py
+++ b/solution.py
@@ -163,7 +163,7 @@
             ],
         ),
         compiler_params=pltpu.CompilerParams(
-            dimension_semantics=("arbitrary",), vmem_limit_bytes=32 * 1024 * 1024
+            dimension_semantics=("arbitrary",), vmem_limit_bytes=56 * 1024 * 1024
         ),
         cost_estimate=pl.CostEstimate(
             flops=4 * pool_pages * page_size * channels * ROWS,
@@ -175,41 +175,46 @@
     return out[:, :heads]
 
 
-def pack_kernel(page_ref, len_ref, *refs):
-    pages = MIGP
-    out_ref = refs[2 * pages]
+def pack_kernel(count, page_ref, len_ref, *refs):
+    outs = refs[2 * MIGP :]
+    step = pl.program_id(0)
     page_size = refs[0].shape[1]
     row = lax.broadcasted_iota(jnp.int32, refs[0].shape[1:], 0)
-    for side in range(2):
-        for t in range(pages):
-            block = refs[side * pages + t][0]
-            keep = row + t * page_size < len_ref[0]
-            out_ref[side, t * page_size : (t + 1) * page_size] = jnp.where(
-                keep, block, jnp.zeros_like(block)
-            )
-
-
-def pack_block(pages, length, k_pool, v_pool):
+    for s in range(count):
+
+        @pl.when(step == s)
+        def _():
+            for side in range(2):
+                for t in range(MIGP):
+                    block = refs[side * MIGP + t][0]
+                    keep = row + t * page_size < len_ref[s]
+                    outs[s][side, t * page_size : (t + 1) * page_size] = jnp.where(
+                        keep, block, jnp.zeros_like(block)
+                    )
+
+
+def pack_blocks(pages, lengths, k_pool, v_pool):
     _, page_size, channels = k_pool.shape
+    count = lengths.shape[0]
     span = MIGP * page_size
 
     def page_spec(t):
-        return pl.BlockSpec((1, page_size, channels), lambda i, page_ref, len_ref: (page_ref[t], 0, 0))
+        return pl.BlockSpec(
+            (1, page_size, channels), lambda i, page_ref, len_ref: (page_ref[i * MIGP + t], 0, 0)
+        )
 
     return pl.pallas_call(
-        pack_kernel,
-        out_shape=jax.ShapeDtypeStruct((2, span, channels), jnp.bfloat16),
+        functools.partial(pack_kernel, count),
+        out_shape=[jax.ShapeDtypeStruct((2, span, channels), jnp.bfloat16)] * count,
         grid_spec=pltpu.PrefetchScalarGridSpec(
             num_scalar_prefetch=2,
-            grid=(1,),
+            grid=(count,),
             in_specs=[page_spec(t) for _ in range(2) for t in range(MIGP)],
-            out_specs=pl.BlockSpec((2, span, channels), lambda i, *_: (0, 0, 0)),
-        ),
-        cost_estimate=pl.CostEstimate(
-            flops=0, bytes_accessed=8 * span * channels, transcendentals=0
-        ),
-        name="pack_block",
-    )(pages, length, *([k_pool] * MIGP), *([v_pool] * MIGP))
+            out_specs=[pl.BlockSpec((2, span, channels), lambda i, *_: (0, 0, 0))] * count,
+        ),
+        compiler_params=pltpu.CompilerParams(vmem_limit_bytes=48 * 1024 * 1024),
+        name="pack_blocks",
+    )(pages.reshape(-1), lengths, *([k_pool] * MIGP), *([v_pool] * MIGP))
 
 
 def place_kernel(count, where_ref, len_ref, fresh_ref, *refs):
@@ -237,6 +242,259 @@
         compiler_params=pltpu.CompilerParams(vmem_limit_bytes=40 * 1024 * 1024),
         name="place_blocks",
     )(where, lengths, fresh, *blocks)
+
+
+def greet(peers):
+    barrier = pltpu.get_barrier_semaphore()
+    for peer in peers:
+        pl.semaphore_signal(
+            barrier, inc=1, device_id=peer, device_id_type=pl.DeviceIdType.MESH
+        )
+    pl.semaphore_wait(barrier, len(peers))
+
+
+def send(source, target, send_sem, recv_sem, peer):
+    copy = pltpu.make_async_remote_copy(
+        src_ref=source,
+        dst_ref=target,
+        send_sem=send_sem,
+        recv_sem=recv_sem,
+        device_id=peer,
+        device_id_type=pl.DeviceIdType.MESH,
+    )
+    copy.start()
+    return copy
+
+
+def ring(axis, n):
+    me = lax.axis_index(axis)
+    return [{axis: lax.rem(me + d, n)} for d in range(1, n)]
+
+
+def row_norm(pieces, gain_ref, out_ref):
+    width = pieces.shape[2]
+    n = pieces.shape[0]
+    squares = 0.0
+    for k in range(n):
+        block = pieces[k].astype(jnp.float32)
+        squares = squares + jnp.sum(block * block, axis=-1, keepdims=True)
+    factor = lax.rsqrt(squares / (n * width) + EPSILON)
+    for k in range(n):
+        cols = slice(k * width, (k + 1) * width)
+        block = pieces[k].astype(jnp.float32)
+        out_ref[:, cols] = (block * factor * gain_ref[:, cols]).astype(out_ref.dtype)
+
+
+def norm_kernel(n, hidden_ref, gain_ref, out_ref, pieces, send_sem, recv_sem):
+    me = lax.axis_index("kv")
+    peers = ring("kv", n)
+    greet(peers)
+    copies = [
+        send(hidden_ref, pieces.at[me], send_sem.at[d], recv_sem.at[d], peer)
+        for d, peer in enumerate(peers)
+    ]
+    pieces[me] = hidden_ref[...]
+    for copy in copies:
+        copy.wait()
+    row_norm(pieces, gain_ref, out_ref)
+
+
+def gathered_norm(hidden, gain, n):
+    rows, width = hidden.shape
+    return pl.pallas_call(
+        functools.partial(norm_kernel, n),
+        out_shape=jax.ShapeDtypeStruct((rows, n * width), jnp.bfloat16),
+        in_specs=[pl.BlockSpec(memory_space=pltpu.VMEM)] * 2,
+        out_specs=pl.BlockSpec(memory_space=pltpu.VMEM),
+        scratch_shapes=[
+            pltpu.VMEM((n, rows, width), jnp.bfloat16),
+            pltpu.SemaphoreType.DMA((n - 1,)),
+            pltpu.SemaphoreType.DMA((n - 1,)),
+        ],
+        compiler_params=pltpu.CompilerParams(collective_id=0, has_side_effects=True),
+        name="gathered_norm",
+    )(hidden, gain[None])
+
+
+def merge_kernel(
+    n, groups, gated_ref, w_ref, hidden_ref, gain_ref, notes_ref,
+    mid_ref, normed_ref, got_ref,
+    parts, came, mids, got, part_s, part_r, mid_s, mid_r, note_s, note_r,
+):
+    me = lax.axis_index("kv")
+    mine = lax.axis_index("req")
+    width = hidden_ref.shape[1]
+    peers = ring("kv", n)
+    others = ring("req", groups)
+    greet(peers + others)
+    copies = []
+    for d, peer in enumerate(others):
+        copies.append(
+            send(notes_ref.at[peer["req"]], got.at[mine], note_s.at[d], note_r.at[d], peer)
+        )
+    got[mine] = notes_ref[mine]
+
+    def part(k):
+        cols = pl.ds(pl.multiple_of(k * width, 128), width)
+        return jnp.dot(gated_ref[...], w_ref[:, cols], preferred_element_type=jnp.float32)
+
+    part_copies = []
+    for d, peer in enumerate(peers):
+        parts[d] = part(peer["kv"]).astype(parts.dtype)
+        part_copies.append(send(parts.at[d], came.at[d], part_s.at[d], part_r.at[d], peer))
+    total = hidden_ref[...].astype(jnp.float32) + part(me)
+    for d, copy in enumerate(part_copies):
+        copy.wait()
+        total = total + came[d].astype(jnp.float32)
+    mid_ref[...] = total.astype(mid_ref.dtype)
+    mids[me] = total.astype(mid_ref.dtype)
+    mid_copies = [
+        send(mid_ref, mids.at[me], mid_s.at[d], mid_r.at[d], peer) for d, peer in enumerate(peers)
+    ]
+    for copy in mid_copies:
+        copy.wait()
+    row_norm(mids, gain_ref, normed_ref)
+    for copy in copies:
+        copy.wait()
+    got_ref[...] = got[...]
+
+
+def merged_norm(gated, w_o, hidden, gain, notes, n, groups):
+    rows, width = hidden.shape
+    dma = pltpu.SemaphoreType.DMA
+    vmem = pl.BlockSpec(memory_space=pltpu.VMEM)
+    return pl.pallas_call(
+        functools.partial(merge_kernel, n, groups),
+        out_shape=(
+            jax.ShapeDtypeStruct((rows, width), jnp.bfloat16),
+            jax.ShapeDtypeStruct((rows, n * width), jnp.bfloat16),
+            jax.ShapeDtypeStruct(notes.shape, notes.dtype),
+        ),
+        in_specs=[vmem] * 5,
+        out_specs=(vmem,) * 3,
+        scratch_shapes=[
+            pltpu.VMEM((n - 1, rows, width), jnp.bfloat16),
+            pltpu.VMEM((n - 1, rows, width), jnp.bfloat16),
+            pltpu.VMEM((n, rows, width), jnp.bfloat16),
+            pltpu.VMEM(notes.shape, notes.dtype),
+            dma((n - 1,)), dma((n - 1,)), dma((n - 1,)), dma((n - 1,)),
+            dma((groups - 1,)), dma((groups - 1,)),
+        ],
+        compiler_params=pltpu.CompilerParams(
+            collective_id=1, has_side_effects=True, vmem_limit_bytes=32 * 1024 * 1024
+        ),
+        name="merged_norm",
+    )(gated, w_o, hidden, gain[None], notes)
+
+
+def mlp_kernel(
+    n, groups, normed_ref, gate_ref, up_ref, down_ref, mid_ref, out_ref,
+    rows, own, pair_out, pair_in, chip_out, chip_in, line_out, line_in,
+    a_s, a_r, b_s, b_r, p_s, p_r, c_s, c_r, z_s, z_r,
+):
+    me = lax.axis_index("req")
+    kv = lax.axis_index("kv")
+    pairs = groups // 2
+    pair, core = me // 2, lax.rem(me, 2)
+    sibling = {"req": pair * 2 + 1 - core}
+    peers = ring("kv", n)
+    far = [{"req": lax.rem(pair + d, pairs) * 2 + core} for d in range(1, pairs)]
+    greet(peers + far + [sibling])
+    count, width = mid_ref.shape
+
+    def at(d):
+        return lax.rem(pair - d + pairs, pairs)
+
+    far_copies = [
+        send(normed_ref, rows.at[me], a_s.at[d], a_r.at[d], peer) for d, peer in enumerate(far)
+    ]
+    forwards = [send(normed_ref, rows.at[me], b_s.at[0], b_r.at[0], sibling)]
+    rows[me] = normed_ref[...]
+    pair_copies = []
+    chip_copies = []
+
+    def reduce(d):
+        pair_copies[d].wait()
+        total = own[d] + pair_in[d].astype(jnp.float32)
+        if d == 0:
+            own[0] = total
+            return
+        chip_out[d - 1] = total.astype(chip_out.dtype)
+        target = {"req": at(d) * 2 + core}
+        chip_copies.append(
+            send(chip_out.at[d - 1], chip_in.at[d - 1], c_s.at[d - 1], c_r.at[d - 1], target)
+        )
+
+    for d in range(pairs):
+        if d > 0:
+            far_copies[d - 1].wait()
+            held = rows.at[at(d) * 2 + core]
+            forwards.append(send(held, held, b_s.at[d], b_r.at[d], sibling))
+        forwards[d].wait()
+        block = rows[pl.ds(at(d) * 2, 2)].reshape(2 * count, n * width)
+        gate = jnp.dot(block, gate_ref[...], preferred_element_type=jnp.float32)
+        up = jnp.dot(block, up_ref[...], preferred_element_type=jnp.float32)
+        act = (gate / (1.0 + jnp.exp(-gate)) * up).astype(jnp.bfloat16)
+        term = lax.dot_general(
+            act, down_ref[...], (((1,), (1,)), ((), ())), preferred_element_type=jnp.float32
+        )
+        low, high = term[:count], term[count:]
+        own[d] = jnp.where(core == 0, low, high)
+        pair_out[d] = jnp.where(core == 0, high, low).astype(pair_out.dtype)
+        pair_copies.append(
+            send(pair_out.at[d], pair_in.at[d], p_s.at[d], p_r.at[d], sibling)
+        )
+        if d > 0:
+            reduce(d - 1)
+    reduce(pairs - 1)
+    for d, copy in enumerate(chip_copies):
+        copy.wait()
+        own[0] = own[0] + chip_in[d].astype(jnp.float32)
+    line_copies = []
+    for d, peer in enumerate(peers):
+        cols = pl.ds(pl.multiple_of(peer["kv"] * width, 128), width)
+        line_out[d] = own[0, :, cols].astype(line_out.dtype)
+        line_copies.append(send(line_out.at[d], line_in.at[d], z_s.at[d], z_r.at[d], peer))
+    total = mid_ref[...].astype(jnp.float32)
+    total = total + own[0, :, pl.ds(pl.multiple_of(kv * width, 128), width)]
+    for d, copy in enumerate(line_copies):
+        copy.wait()
+        total = total + line_in[d].astype(jnp.float32)
+    out_ref[...] = total.astype(out_ref.dtype)
+
+
+def mlp(normed, w_gate, w_up, w_down, mid, n, groups):
+    rows, width = mid.shape
+    pairs = groups // 2
+    wide = n * width
+    dma = pltpu.SemaphoreType.DMA
+    vmem = pl.BlockSpec(memory_space=pltpu.VMEM)
+    half = jnp.bfloat16
+    return pl.pallas_call(
+        functools.partial(mlp_kernel, n, groups),
+        out_shape=jax.ShapeDtypeStruct((rows, width), half),
+        in_specs=[vmem] * 5,
+        out_specs=vmem,
+        scratch_shapes=[
+            pltpu.VMEM((groups, rows, wide), half),
+            pltpu.VMEM((pairs, rows, wide), jnp.float32),
+            pltpu.VMEM((pairs, rows, wide), half),
+            pltpu.VMEM((pairs, rows, wide), half),
+            pltpu.VMEM((pairs - 1, rows, wide), half),
+            pltpu.VMEM((pairs - 1, rows, wide), half),
+            pltpu.VMEM((n - 1, rows, width), half),
+            pltpu.VMEM((n - 1, rows, width), half),
+            dma((pairs - 1,)), dma((pairs - 1,)),
+            dma((pairs,)), dma((pairs,)),
+            dma((pairs,)), dma((pairs,)),
+            dma((pairs - 1,)), dma((pairs - 1,)),
+            dma((n - 1,)), dma((n - 1,)),
+        ],
+        compiler_params=pltpu.CompilerParams(
+            collective_id=2, has_side_effects=True, vmem_limit_bytes=48 * 1024 * 1024
+        ),
+        name="mlp_exchange",
+    )(normed, w_gate, w_up, w_down, mid)
 
 
 def per_device(
@@ -266,7 +524,6 @@
     q_local = w_q.shape[1] // head_dim
     group_size = q_local // kv_local
     channels = kv_local * head_dim
-    model_width = mlp_gain.shape[0]
     req_groups = lax.axis_size("req")
     me = lax.axis_index("req")
 
@@ -277,16 +534,15 @@
     send_rows = jnp.sum(jnp.where(chosen, mig_rows[None, :], 0), axis=1)
     send_len = lengths[send_rows]
     send_pages = page_table[send_rows, :MIGP]
-    packed = [
-        pack_block(send_pages[s], send_len[s : s + 1], k_pool, v_pool) for s in range(req_groups)
-    ]
+    kv_count = lax.axis_size("kv")
+    packed = pack_blocks(send_pages, send_len, k_pool, v_pool)
+    packed, hidden = lax.optimization_barrier((packed, hidden))
     arrived = [packed[0]] + [
         lax.ppermute(packed[s], "req", [(i, i ^ s) for i in range(req_groups)])
         for s in range(1, req_groups)
     ]
 
-    whole_rows = lax.all_gather(hidden, "kv", axis=1, tiled=True)
-    normed = rms_norm(whole_rows, attn_gain).astype(jnp.bfloat16)
+    normed = gathered_norm(hidden, attn_gain, kv_count)
     query_raw = jnp.dot(normed, w_q, preferred_element_type=jnp.float32).reshape(
         req_count, q_local, head_dim
     )
@@ -313,41 +569,27 @@
         ),
         axis=1,
     )
-    dest_len = lengths[by_dest]
-    digits = jnp.stack([dest_len // 256, dest_len % 256], axis=1).astype(jnp.bfloat16)
-    notes = jnp.concatenate([fresh[by_dest], jnp.pad(digits, ((0, 0), (0, 126)))], axis=1)
-    all_notes = lax.all_gather(notes, "req", axis=0, tiled=False)
-    mine = lax.dynamic_index_in_dim(all_notes, me, 1, keepdims=False)[partner]
+    dest_len = lengths[by_dest].astype(jnp.float32)
     width = 2 * channels
-    got_digits = mine[:, width : width + 2].astype(jnp.int32)
-    got_len = got_digits[:, 0] * 256 + got_digits[:, 1]
-    mig_keys, mig_values = place_blocks(partner, got_len, mine[:, None, :width], arrived)
-
+    notes = jnp.concatenate(
+        [fresh[by_dest].astype(jnp.float32), jnp.broadcast_to(dest_len[:, None], (req_groups, 128))],
+        axis=1,
+    )
+    notes = jnp.broadcast_to(notes[:, None, :], (req_groups, 8, width + 128))
     context = attend(queries, new_keys, new_values, k_pool, v_pool, lengths, page_table)
     gated = (jax.nn.sigmoid(gate_raw) * context.reshape(req_count, q_local * head_dim)).astype(
         jnp.bfloat16
     )
-    head_terms = jnp.dot(gated, w_o, preferred_element_type=jnp.float32)
-    attn_sum = lax.psum(head_terms, "kv")
-    mid_stream = (whole_rows.astype(jnp.float32) + attn_sum).astype(jnp.bfloat16)
-    normed_mlp = rms_norm(mid_stream, mlp_gain).astype(jnp.bfloat16)
-    kv_count = lax.axis_size("kv")
-    slice_width = model_width // kv_count
-    slice_start = lax.axis_index("kv") * slice_width
-    mid_slice = lax.dynamic_slice_in_dim(mid_stream, slice_start, slice_width, 1)
-    row_piece = lax.all_gather(normed_mlp, "req", axis=0, tiled=True)
-    gate_part = jnp.dot(row_piece, w_gate, preferred_element_type=jnp.float32)
-    up_part = jnp.dot(row_piece, w_up, preferred_element_type=jnp.float32)
-    activation = (jax.nn.silu(gate_part) * up_part).astype(jnp.bfloat16)
-    unit_count = activation.shape[1]
-    grouped_act = activation.reshape(req_groups, req_count, unit_count)
-    grouped_down = w_down.reshape(kv_count, slice_width, unit_count)
-    term = jnp.einsum(
-        "gru,hcu->ghrc", grouped_act, grouped_down, preferred_element_type=jnp.float32
-    )
-    term = term.reshape(req_groups * kv_count, req_count, slice_width)
-    mlp_part = lax.psum_scatter(term, ("req", "kv"), scatter_dimension=0, tiled=True)[0]
-    out_hidden = (mid_slice.astype(jnp.float32) + mlp_part).astype(jnp.bfloat16)
+    mid_slice, normed_mlp, got = merged_norm(
+        gated, w_o, hidden, mlp_gain, notes, kv_count, req_groups
+    )
+    arrived, normed_mlp = lax.optimization_barrier((arrived, normed_mlp))
+    mine = got[partner, 0]
+    got_len = mine[:, width].astype(jnp.int32)
+    mig_keys, mig_values = place_blocks(
+        partner, got_len, mine[:, None, :width].astype(jnp.bfloat16), arrived
+    )
+    out_hidden = mlp(normed_mlp, w_gate, w_up, w_down, mid_slice, kv_count, req_groups)
     return (out_hidden, mig_keys, mig_values)
 
 

time: 297 us -> 161 us (0.54)
  waiting for transfers between devices: 143 us -> 0.02 us
  Pallas kernels: 38 us -> 108 us
  blocking collectives: 43 us -> 0 us
  between operations: 14.2 us -> 1.07 us
  matrix products: 15 us -> 5.65 us
  local copies, waits for them, and re-layouts: 23.3 us -> 30.1 us
  other arithmetic: 12.9 us -> 7.43 us
    pallas_call x8 -> x4, Pallas kernels: 25.8 us -> 84.5 us  [the longest x1 40.3 us: mlp(): pl.pallas_call(functools.partial(mlp_kernel, n, groups), out_shape=jax.Sh...]
    reduce_scatter x1 -> x0, waiting for transfers between devices: 50.7 us -> none  [per_device(): lax.psum_scatter(term, ('req', 'kv'), scatter_dimension=0, tiled=True)[0]]
    all_gather x2 -> x0, blocking collectives: 43 us -> none  [the longest x1 27.2 us: per_device(): all_notes = lax.all_gather(notes, 'req', axis=0, tiled=False)]
    psum x1 -> x0, waiting for transfers between devices: 39.9 us -> none  [per_device(): attn_sum = lax.psum(head_terms, 'kv')]
    all_gather x1 -> x0, waiting for transfers between devices: 28 us -> none  [per_device(): row_piece = lax.all_gather(normed_mlp, 'req', axis=0, tiled=True)]
    ppermute x7, waiting for transfers between devices: 24.1 us -> 0.02 us  [per_device(): lax.ppermute(packed[s], 'req', [(i, i ^ s) for i in range(req_groups)])]
    pallas_call x1, Pallas kernels: 7.92 us -> 18.8 us  [attend(): pl.pallas_call(functools.partial(attend_kernel, slots, group, blocks, per...]
    dot_general x4 -> x1, matrix products: 10.8 us -> 2.25 us  [per_device(): gate_raw = jnp.dot(normed, w_gate_attn, preferred_element_type=jnp.float32)]
  transfers between devices with their start and end apart: 10 -> 7, of which waited for: 5 -> 0; matrix products, arithmetic and copies ran while one was open for 3% -> 18% of each run, Pallas kernels for 10% -> 35%
where the time goes in v2:
time: 161 us; the launch traced here: 159 us
  Pallas kernels  108 us (67%)
  local copies, waits for them, and re-layouts  30.1 us (19%)
  other arithmetic  7.43 us (5%)
  starting transfers between devices  7.4 us (5%)
  matrix products  5.65 us (4%)
    pallas_call x1, Pallas kernels, mlp(): pl.pallas_call(functools.partial(mlp_kernel, n, groups), out_shape=jax.Sh...  40.3 us
    pallas_call x1, Pallas kernels, merged_norm(): pl.pallas_call(functools.partial(merge_kernel, n, groups), out_shape=(jax...  25.7 us
    pallas_call x1, Pallas kernels, attend(): pl.pallas_call(functools.partial(attend_kernel, slots, group, blocks, per...  18.8 us
    unnamed x47, local copies, waits for them, and re-layouts  12.1 us
    pallas_call x1, Pallas kernels, gathered_norm(): pl.pallas_call(functools.partial(norm_kernel, n), out_shape=jax.ShapeDtyp...  11.1 us
    ppermute x7, starting transfers between devices, per_device(): lax.ppermute(packed[s], 'req', [(i, i ^ s) for i in range(req_groups)])  7.4 us
    pallas_call x1, Pallas kernels, pack_blocks(): pl.pallas_call(functools.partial(pack_kernel, count), out_shape=[jax.Shap...  7.27 us
    gather x5, local copies, waits for them, and re-layouts, per_device(): send_pages = page_table[send_rows, :MIGP]  5.55 us
  transfers between devices with their start and end apart: 7, of which 0 were waited for; matrix products, arithmetic and copies ran while one was open for 18% of the time, Pallas kernels for 35%

profile of v2, /device:TPU:0, one launch (start us, length us, event | category | flops | bytes accessed | tf_op | source)
XLA Modules:
  0.0 159.5 jit_solution(10226676096799786548)
XLA Ops:
  0.7 1.6 select_reduce_fusion.1
  3.0 1.4 gather_fusion.7
  4.3 1.4 gather_fusion.6
  5.7 1.4 gather_fusion.5
  7.1 1.4 gather_fusion.4
  9.3 7.3 %pack_blocks.1 = (bf16[2,512,256]{2,1,0:T(8,128)(2,1)S(1)}, bf16[2,512,256]{2,1,0:T(8,128)(2,1)}, bf16[2,512,256]{2,1,0:T(8,128)(2,1)}, bf16[2,512,256]{2,1,0:T(...) custom-call(s32[32]{0:T(128)S(1)} %reshape.197.page_ref, ...), custom_call_target="tpu_custom_call" | custom-call | tf_op jit(solution)/shard_map/pack_blocks/pallas_call | solution.py:206
  19.4 2.4 %collective-permute-start.1 = (bf16[2,512,256]{2,1,0:T(8,128)(2,1)}, bf16[2,512,256]{2,1,0:T(8,128)(2,1)}, u32[]{:S(2)}, u32[]{:S(2)}) collective-permute-start(bf16[2,512,256]{2,1,0:T(8,128)(2,1)} %get-tuple-element.44), channel_id=1, source_target_pairs={{0,8},{4,12},{8,0},{12,4},{16,24},{20,28},{24,16},{28,20},{1,9},{5... | collective-permute-start | bytes 1572872 | tf_op jit(solution)/shard_map/ppermute | solution.py:541
  21.9 2.0 %collective-permute-start.3 = (bf16[2,512,256]{2,1,0:T(8,128)(2,1)}, bf16[2,512,256]{2,1,0:T(8,128)(2,1)}, u32[]{:S(2)}, u32[]{:S(2)}) collective-permute-start(bf16[2,512,256]{2,1,0:T(8,128)(2,1)} %get-tuple-element.46), channel_id=1, source_target_pairs={{0,16},{4,20},{8,24},{12,28},{16,0},{20,4},{24,8},{28,12},{1,17},{... | collective-permute-start | bytes 1572872 | tf_op jit(solution)/shard_map/ppermute | solution.py:541
  26.0 11.1 %gathered_norm.1 = bf16[64,2048]{1,0:T(8,128)(2,1)} custom-call(bf16[64,512]{1,0:T(8,128)(2,1)} %hidden_ref.1, f32[1,2048]{1,0:T(1,128)} %bitcast.70), custom_call_target="tpu_custom_call" | custom-call | tf_op jit(solution)/shard_map/gathered_norm/pallas_call | solution.py:304
  37.2 2.2 %fusion.14 = f32[64,512]{1,0:T(8,128)} fusion(bf16[64,2048]{1,0:T(8,128)(2,1)} %gathered_norm.1, bf16[2048,512]{1,0:T(8,128)(2,1)S(1)} %copy-done), kind=kOutput, calls=%fused_computation.72 | convolution fusion | flops 134217728 | bytes 2490368 | tf_op jit(solution)/shard_map/dot_general | solution.py:546
  42.7 1.9 %mul.163 = f32[64,4,256]{2,1,0:T(4,128)} reshape(f32[64,2,2,2,128]{4,3,2,1,0:T(2,128)} %mul.162) | data formatting | bytes 524288 | tf_op jit(solution)/shard_map/mul | solution.py:124
  50.9 18.8 %attend_pool.1 = f32[64,8,128]{2,1,0:T(8,128)} custom-call(s32[150]{0:T(256)} %select_reduce_fusion.code_ref, s32[64]{0:T(128)} %len_ref.1, f32[64,8,256]{2,1,0:T(8,128)} %pad.13.q_ref, f32[64,8,128]{2,1,0:T(8,128)} %pad.14.k_new_ref, f32[64,8,128]{2,1,0:T(8,128)} %pad.15.v_new_ref, bf16[150,128,256]{2,1,0:T(8,128)(2,1)} %k_ref.1, bf16[150,128,256]{2,1,0:T(8,128)(2,1)} %v_ref.1), custom_call_target="tpu_custom_call" | custom-call | flops 157286400 | bytes 19660800 | tf_op jit(solution)/shard_map/attend_pool/pallas_call | solution.py:136
  69.7 1.6 %slice.49 = f32[64,4,128]{2,1,0:T(4,128)} slice(f32[64,8,128]{2,1,0:T(8,128)} %attend_pool.1), slice={[0:64], [0:4], [0:128]} | slice | bytes 262144 | tf_op jit(solution)/shard_map/slice | solution.py:175
  72.6 1.4 copy.52.gate_ref
  74.1 2.2 %copy.53.up_ref = bf16[2048,192]{1,0:T(8,128)(2,1)} copy(bf16[2048,192]{0,1:T(8,128)(2,1)} %param.36) | data formatting | bytes 1572864 | tf_op args[17]
  76.3 2.2 %copy.54.down_ref = bf16[2048,192]{1,0:T(8,128)(2,1)} copy(bf16[2048,192]{0,1:T(8,128)(2,1)} %param.37) | data formatting | bytes 1572864 | tf_op args[18]
  78.5 2.2 %fusion.4.gated_ref = bf16[64,512]{1,0:T(8,128)(2,1)S(1)} fusion(bf16[64,2048]{1,0:T(8,128)(2,1)S(1)} %copy-done.14, bf16[2048,512]{1,0:T(8,128)(2,1)} %param.24, f32[8,8,4,128]{3,2,1,0:T(4,128)} %bitcast.60), kind=kOutput, calls=%fused_computation.15 | convolution fusion | flops 134381568 | bytes 2555904 | tf_op jit(solution)/shard_map/dot_general | solution.py:549
  80.8 2.4 %collective-permute-start.5 = (bf16[2,512,256]{2,1,0:T(8,128)(2,1)}, bf16[2,512,256]{2,1,0:T(8,128)(2,1)}, u32[]{:S(2)}, u32[]{:S(2)}) collective-permute-start(bf16[2,512,256]{2,1,0:T(8,128)(2,1)} %copy-done.10), channel_id=1, source_target_pairs={{0,24},{4,28},{8,16},{12,20},{16,8},{20,12},{24,0},{28,4},{1,25},{... | collective-permute-start | bytes 1572872 | tf_op jit(solution)/shard_map/ppermute | solution.py:541
  83.4 25.7 %merged_norm.1 = (bf16[64,512]{1,0:T(8,128)(2,1)S(1)}, bf16[64,2048]{1,0:T(8,128)(2,1)S(1)}, f32[8,8,640]{2,1,0:T(8,128)S(1)}) custom-call(bf16[64,512]{1,0:T(8,128)(2,1)S(1)} %fusion.4.gated_ref, bf16[512,2048]{1,0:T(8,128)(2,1)S(1)} %copy-done.3, bf16[64,512]{1,0:T(8,128)(2,1)S(1)} %copy-done.6, f32[1,2048]{1,0:T(1,128)S(1)} %bitcast.57, ...), custom_call_target="tpu_custom_call" | custom-call | tf_op jit(solution)/shard_map/merged_norm/pallas_call | solution.py:366
  109.8 1.5 gather_fusion.3
  111.5 1.2 copy-done.1
  112.7 1.2 copy-done.2
  114.0 40.3 %mlp_exchange.1 = bf16[64,512]{1,0:T(8,128)(2,1)S(1)} custom-call(bf16[64,2048]{1,0:T(8,128)(2,1)S(1)} %get-tuple-element.52.normed_ref, bf16[2048,192]{1,0:T(8,128)(2,1)S(1)} %copy.52.gate_ref, bf16[2048,192]{1,0:T(8,128)(2,1)S(1)} %copy-done.1, bf16[2048,192]{1,0:T(8,128)(2,1)S(1)} %copy-done.2, bf16[64,512]{1,0:T(8,128)(2,1)S(1)} %get-tuple-element.53.mid_ref), custom_call_target="tpu_custom_call" | custom-call | tf_op jit(solution)/shard_map/mlp_exchange/pallas_call | solution.py:473
  154.3 4.6 %place_blocks.1 = (bf16[8,512,256]{2,1,0:T(8,128)(2,1)}, bf16[8,512,256]{2,1,0:T(8,128)(2,1)}) custom-call(s32[8]{0:T(128)S(1)} %iota_xor_fusion.where_ref, s32[8]{0:T(128)S(1)} %fusion.7.len_ref, bf16[8,1,512]{2,1,0:T(2,128)(2,1)S(1)} %copy.55.fresh_ref, bf16[2,512,256]{2,1,0:T(8,128)(2,1)S(1)} %copy-done.5, ...), custom_call_target="tpu_custom_call" | custom-call | tf_op jit(solution)/shard_map/place_blocks/pallas_call | solution.py:237
  (109 shorter events, 18.9 us)
Async XLA Ops:
  0.6 36.5 %copy-start = (bf16[2048,512]{1,0:T(8,128)(2,1)S(1)}, bf16[2048,512]{1,0:T(8,128)(2,1)}, u32[]{:S(2)}) copy-start(bf16[2048,512]{1,0:T(8,128)(2,1)} %param.23) | copy-start | bytes 6291460
  0.6 8.0 %copy-start.11 = (s32[64]{0:T(128)S(1)}, s32[64]{0:T(128)}, u32[]{:S(2)}) copy-start(s32[64]{0:T(128)} %len_ref.1) | copy-start | bytes 772
  9.3 15.7 %copy-start.13 = (s32[64,32]{0,1:T(8,128)S(1)}, s32[64,32]{0,1:T(8,128)}, u32[]{:S(2)}) copy-start(s32[64,32]{0,1:T(8,128)} %param.31) | copy-start | bytes 24580
  16.6 0.8 copy-start.4
  19.0 21.5 %copy-start.17 = (f32[128]{0:T(128)S(1)}, f32[128]{0:T(128)}, u32[]{:S(2)}) copy-start(f32[128]{0:T(128)} %param.21) | copy-start | bytes 1540
  19.0 61.8 %collective-permute-start = (bf16[2,512,256]{2,1,0:T(8,128)(2,1)}, bf16[2,512,256]{2,1,0:T(8,128)(2,1)}, u32[]{:S(2)}, u32[]{:S(2)}) collective-permute-start(bf16[2,512,256]{2,1,0:T(8,128)(2,1)} %get-tuple-element.43), channel_id=1, source_target_pairs={{0,4},{4,0},{8,12},{12,8},{16,20},{20,16},{24,28},{28,24},{1,5},{5... | collective-permute-start | bytes 1572872 | tf_op jit(solution)/shard_map/ppermute | solution.py:541
  19.4 63.9 %collective-permute-start.1 = (bf16[2,512,256]{2,1,0:T(8,128)(2,1)}, bf16[2,512,256]{2,1,0:T(8,128)(2,1)}, u32[]{:S(2)}, u32[]{:S(2)}) collective-permute-start(bf16[2,512,256]{2,1,0:T(8,128)(2,1)} %get-tuple-element.44), channel_id=1, source_target_pairs={{0,8},{4,12},{8,0},{12,4},{16,24},{20,28},{24,16},{28,20},{1,9},{5... | collective-permute-start | bytes 1572872 | tf_op jit(solution)/shard_map/ppermute | solution.py:541
  21.8 89.7 %collective-permute-start.2 = (bf16[2,512,256]{2,1,0:T(8,128)(2,1)}, bf16[2,512,256]{2,1,0:T(8,128)(2,1)}, u32[]{:S(2)}, u32[]{:S(2)}) collective-permute-start(bf16[2,512,256]{2,1,0:T(8,128)(2,1)} %get-tuple-element.45), channel_id=1, source_target_pairs={{0,12},{4,8},{8,4},{12,0},{16,28},{20,24},{24,20},{28,16},{1,13},{... | collective-permute-start | bytes 1572872 | tf_op jit(solution)/shard_map/ppermute | solution.py:541
  21.9 89.5 %collective-permute-start.3 = (bf16[2,512,256]{2,1,0:T(8,128)(2,1)}, bf16[2,512,256]{2,1,0:T(8,128)(2,1)}, u32[]{:S(2)}, u32[]{:S(2)}) collective-permute-start(bf16[2,512,256]{2,1,0:T(8,128)(2,1)} %get-tuple-element.46), channel_id=1, source_target_pairs={{0,16},{4,20},{8,24},{12,28},{16,0},{20,4},{24,8},{28,12},{1,17},{... | collective-permute-start | bytes 1572872 | tf_op jit(solution)/shard_map/ppermute | solution.py:541
  24.0 87.5 %collective-permute-start.4 = (bf16[2,512,256]{2,1,0:T(8,128)(2,1)}, bf16[2,512,256]{2,1,0:T(8,128)(2,1)}, u32[]{:S(2)}, u32[]{:S(2)}) collective-permute-start(bf16[2,512,256]{2,1,0:T(8,128)(2,1)} %get-tuple-element.47), channel_id=1, source_target_pairs={{0,20},{4,16},{8,28},{12,24},{16,4},{20,0},{24,12},{28,8},{1,21},{... | collective-permute-start | bytes 1572872 | tf_op jit(solution)/shard_map/ppermute | solution.py:541
  37.2 7.5 %copy-start.14 = (bf16[64,2048]{1,0:T(8,128)(2,1)S(1)}, bf16[64,2048]{1,0:T(8,128)(2,1)}, u32[]{:S(2)}) copy-start(bf16[64,2048]{1,0:T(8,128)(2,1)} %gathered_norm.1) | copy-start | bytes 786436
  37.2 7.5 %copy-start.15 = (bf16[2048,256]{1,0:T(8,128)(2,1)S(1)}, bf16[2048,256]{1,0:T(8,128)(2,1)}, u32[]{:S(2)}) copy-start(bf16[2048,256]{1,0:T(8,128)(2,1)} %param.25) | copy-start | bytes 3145732
  39.4 7.4 %copy-start.18 = (f32[128]{0:T(128)S(1)}, f32[128]{0:T(128)}, u32[]{:S(2)}) copy-start(f32[128]{0:T(128)} %param.22) | copy-start | bytes 1540
  45.6 4.2 %copy-start.16 = (bf16[2048,256]{1,0:T(8,128)(2,1)S(1)}, bf16[2048,256]{1,0:T(8,128)(2,1)}, u32[]{:S(2)}) copy-start(bf16[2048,256]{1,0:T(8,128)(2,1)} %param.26) | copy-start | bytes 3145732
  46.9 4.0 %copy-start.19 = (s32[8]{0:T(128)S(1)}, s32[8]{0:T(128)}, u32[]{:S(2)}) copy-start(s32[8]{0:T(128)} %get-tuple-element.65) | copy-start | bytes 100
  50.9 20.4 %copy-start.12 = (s32[64]{0:T(128)S(1)}, s32[64]{0:T(128)}, u32[]{:S(2)}) copy-start(s32[64]{0:T(128)} %len_ref.1) | copy-start | bytes 772
  76.3 7.1 %copy-start.6 = (bf16[64,512]{1,0:T(8,128)(2,1)S(1)}, bf16[64,512]{1,0:T(8,128)(2,1)}, u32[]{:S(2)}) copy-start(bf16[64,512]{1,0:T(8,128)(2,1)} %hidden_ref.1) | copy-start | bytes 196612
  76.3 7.1 %copy-start.8 = (f32[2048]{0:T(1024)S(1)}, f32[2048]{0:T(1024)}, u32[]{:S(2)}) copy-start(f32[2048]{0:T(1024)} %param.34) | copy-start | bytes 24580
  78.5 4.8 %copy-start.3 = (bf16[512,2048]{1,0:T(8,128)(2,1)S(1)}, bf16[512,2048]{1,0:T(8,128)(2,1)}, u32[]{:S(2)}) copy-start(bf16[512,2048]{1,0:T(8,128)(2,1)} %w_ref.1) | copy-start | bytes 6291460
  80.8 30.7 %collective-permute-start.5 = (bf16[2,512,256]{2,1,0:T(8,128)(2,1)}, bf16[2,512,256]{2,1,0:T(8,128)(2,1)}, u32[]{:S(2)}, u32[]{:S(2)}) collective-permute-start(bf16[2,512,256]{2,1,0:T(8,128)(2,1)} %copy-done.10), channel_id=1, source_target_pairs={{0,24},{4,28},{8,16},{12,20},{16,8},{20,12},{24,0},{28,4},{1,25},{... | collective-permute-start | bytes 1572872 | tf_op jit(solution)/shard_map/ppermute | solution.py:541
  83.2 28.3 %collective-permute-start.6 = (bf16[2,512,256]{2,1,0:T(8,128)(2,1)}, bf16[2,512,256]{2,1,0:T(8,128)(2,1)}, u32[]{:S(2)}, u32[]{:S(2)}) collective-permute-start(bf16[2,512,256]{2,1,0:T(8,128)(2,1)} %copy-done.9), channel_id=1, source_target_pairs={{0,28},{4,24},{8,20},{12,16},{16,12},{20,8},{24,4},{28,0},{1,29},{... | collective-permute-start | bytes 1572872 | tf_op jit(solution)/shard_map/ppermute | solution.py:541
  111.5 1.2 copy-start.1
  112.7 1.2 copy-start.2
  114.0 40.3 %copy-start.5 = (bf16[2,512,256]{2,1,0:T(8,128)(2,1)S(1)}, bf16[2,512,256]{2,1,0:T(8,128)(2,1)}, u32[]{:S(2)}) copy-start(bf16[2,512,256]{2,1,0:T(8,128)(2,1)} %copy-done.4) | copy-start | bytes 1572868
  (3 other events, 2.3 us)

commit v3 on v2

--- a/solution.py
+++ b/solution.py
@@ -47,12 +47,15 @@
 
 def attend_kernel(
     slots, group, blocks, per_block, page_size, scale,
-    code_ref, len_ref, q_ref, k_new_ref, v_new_ref, k_ref, v_ref,
-    out_ref, scores, top, total, acc,
+    code_ref, len_ref, q_ref, k_new_ref, v_new_ref, *refs,
 ):
+    streams = (len(refs) - 5) // 2
+    k_refs, v_refs = refs[:streams], refs[streams : 2 * streams]
+    out_ref, scores, top, total, acc = refs[2 * streams :]
+    each = per_block // streams
     step = pl.program_id(0)
     head_dim = out_ref.shape[-1]
-    kv_local = k_ref.shape[-1] // head_dim
+    kv_local = k_refs[0].shape[-1] // head_dim
     lane = lax.broadcasted_iota(jnp.int32, (ROWS, page_size), 1)
     row = lax.broadcasted_iota(jnp.int32, (ROWS, head_dim), 0)
 
@@ -75,7 +78,7 @@
             left = jnp.where(code < 0, 0, len_ref[owner] - lax.rem(code, slots) * page_size)
             s = lax.dot_general(
                 q_ref[owner].astype(jnp.bfloat16),
-                k_ref[j],
+                k_refs[j // each][j % each],
                 (((1,), (1,)), ((), ())),
                 preferred_element_type=jnp.float32,
             )
@@ -99,7 +102,7 @@
             owner = jnp.maximum(code_ref[page], 0) // slots
             e = jnp.exp(scores[page] - top[owner])
             total[owner] = total[owner] + e
-            o = jnp.dot(e.astype(jnp.bfloat16), v_ref[j], preferred_element_type=jnp.float32)
+            o = jnp.dot(e.astype(jnp.bfloat16), v_refs[j // each][j % each], preferred_element_type=jnp.float32)
             picked = o[:, :head_dim]
             for k in range(1, kv_local):
                 picked = jnp.where(
@@ -131,6 +134,19 @@
         values = jnp.repeat(values.astype(jnp.float32), group, axis=1)
         return jnp.pad(values, pad)
 
+    streams = max(c for c in range(1, 6) if per_block % c == 0)
+    stream_shape = (per_block // streams, page_size, channels)
+
+    def k_spec(t):
+        return pl.BlockSpec(
+            stream_shape, lambda i, *_: (jnp.minimum(i, blocks - 1) * streams + t, 0, 0)
+        )
+
+    def v_spec(t):
+        return pl.BlockSpec(
+            stream_shape, lambda i, *_: (jnp.maximum(i - blocks, 0) * streams + t, 0, 0)
+        )
+
     whole = pl.BlockSpec((req_count, ROWS, channels), lambda i, *_: (0, 0, 0))
     slim = pl.BlockSpec((req_count, ROWS, head_dim), lambda i, *_: (0, 0, 0))
     out = pl.pallas_call(
@@ -145,14 +161,8 @@
                 whole,
                 slim,
                 slim,
-                pl.BlockSpec(
-                    (per_block, page_size, channels),
-                    lambda i, *_: (jnp.minimum(i, blocks - 1), 0, 0),
-                ),
-                pl.BlockSpec(
-                    (per_block, page_size, channels),
-                    lambda i, *_: (jnp.maximum(i - blocks, 0), 0, 0),
-                ),
+                *[k_spec(t) for t in range(streams)],
+                *[v_spec(t) for t in range(streams)],
             ],
             out_specs=slim,
             scratch_shapes=[
@@ -171,11 +181,11 @@
             transcendentals=pool_pages * page_size * ROWS,
         ),
         name="attend_pool",
-    )(code, lengths, spread, by_head(new_keys), by_head(new_values), k_pool, v_pool)
+    )(code, lengths, spread, by_head(new_keys), by_head(new_values), *([k_pool] * streams), *([v_pool] * streams))
     return out[:, :heads]
 
 
-def pack_kernel(count, page_ref, len_ref, *refs):
+def pack_kernel(count, send_ref, page_ref, len_ref, *refs):
     outs = refs[2 * MIGP :]
     step = pl.program_id(0)
     page_size = refs[0].shape[1]
@@ -187,34 +197,35 @@
             for side in range(2):
                 for t in range(MIGP):
                     block = refs[side * MIGP + t][0]
-                    keep = row + t * page_size < len_ref[s]
+                    keep = row + t * page_size < len_ref[send_ref[s]]
                     outs[s][side, t * page_size : (t + 1) * page_size] = jnp.where(
                         keep, block, jnp.zeros_like(block)
                     )
 
 
-def pack_blocks(pages, lengths, k_pool, v_pool):
+def pack_blocks(send_rows, page_table, lengths, k_pool, v_pool):
     _, page_size, channels = k_pool.shape
-    count = lengths.shape[0]
+    count = send_rows.shape[0]
     span = MIGP * page_size
 
     def page_spec(t):
         return pl.BlockSpec(
-            (1, page_size, channels), lambda i, page_ref, len_ref: (page_ref[i * MIGP + t], 0, 0)
+            (1, page_size, channels),
+            lambda i, send_ref, page_ref, len_ref: (page_ref[send_ref[i], t], 0, 0),
         )
 
     return pl.pallas_call(
         functools.partial(pack_kernel, count),
         out_shape=[jax.ShapeDtypeStruct((2, span, channels), jnp.bfloat16)] * count,
         grid_spec=pltpu.PrefetchScalarGridSpec(
-            num_scalar_prefetch=2,
+            num_scalar_prefetch=3,
             grid=(count,),
             in_specs=[page_spec(t) for _ in range(2) for t in range(MIGP)],
             out_specs=[pl.BlockSpec((2, span, channels), lambda i, *_: (0, 0, 0))] * count,
         ),
         compiler_params=pltpu.CompilerParams(vmem_limit_bytes=48 * 1024 * 1024),
         name="pack_blocks",
-    )(pages.reshape(-1), lengths, *([k_pool] * MIGP), *([v_pool] * MIGP))
+    )(send_rows, page_table, lengths, *([k_pool] * MIGP), *([v_pool] * MIGP))
 
 
 def place_kernel(count, where_ref, len_ref, fresh_ref, *refs):
@@ -401,6 +412,7 @@
     far = [{"req": lax.rem(pair + d, pairs) * 2 + core} for d in range(1, pairs)]
     greet(peers + far + [sibling])
     count, width = mid_ref.shape
+    across = (((1,), (1,)), ((), ()))
 
     def at(d):
         return lax.rem(pair - d + pairs, pairs)
@@ -432,12 +444,10 @@
             forwards.append(send(held, held, b_s.at[d], b_r.at[d], sibling))
         forwards[d].wait()
         block = rows[pl.ds(at(d) * 2, 2)].reshape(2 * count, n * width)
-        gate = jnp.dot(block, gate_ref[...], preferred_element_type=jnp.float32)
-        up = jnp.dot(block, up_ref[...], preferred_element_type=jnp.float32)
+        gate = lax.dot_general(block, gate_ref[...], across, preferred_element_type=jnp.float32)
+        up = lax.dot_general(block, up_ref[...], across, preferred_element_type=jnp.float32)
         act = (gate / (1.0 + jnp.exp(-gate)) * up).astype(jnp.bfloat16)
-        term = lax.dot_general(
-            act, down_ref[...], (((1,), (1,)), ((), ())), preferred_element_type=jnp.float32
-        )
+        term = jnp.dot(act, down_ref[...], preferred_element_type=jnp.float32)
         low, high = term[:count], term[count:]
         own[d] = jnp.where(core == 0, low, high)
         pair_out[d] = jnp.where(core == 0, high, low).astype(pair_out.dtype)
@@ -494,7 +504,7 @@
             collective_id=2, has_side_effects=True, vmem_limit_bytes=48 * 1024 * 1024
         ),
         name="mlp_exchange",
-    )(normed, w_gate, w_up, w_down, mid)
+    )(normed, w_gate.T, w_up.T, w_down.T, mid)
 
 
 def per_device(
@@ -532,10 +542,8 @@
     partner = me ^ jnp.arange(req_groups, dtype=jnp.int32)
     chosen = dest_row[None, :] == partner[:, None]
     send_rows = jnp.sum(jnp.where(chosen, mig_rows[None, :], 0), axis=1)
-    send_len = lengths[send_rows]
-    send_pages = page_table[send_rows, :MIGP]
     kv_count = lax.axis_size("kv")
-    packed = pack_blocks(send_pages, send_len, k_pool, v_pool)
+    packed = pack_blocks(send_rows, page_table, lengths, k_pool, v_pool)
     packed, hidden = lax.optimization_barrier((packed, hidden))
     arrived = [packed[0]] + [
         lax.ppermute(packed[s], "req", [(i, i ^ s) for i in range(req_groups)])
@@ -543,6 +551,7 @@
     ]
 
     normed = gathered_norm(hidden, attn_gain, kv_count)
+    normed, arrived[1] = lax.optimization_barrier((normed, arrived[1]))
     query_raw = jnp.dot(normed, w_q, preferred_element_type=jnp.float32).reshape(
         req_count, q_local, head_dim
     )
@@ -577,6 +586,7 @@
     )
     notes = jnp.broadcast_to(notes[:, None, :], (req_groups, 8, width + 128))
     context = attend(queries, new_keys, new_values, k_pool, v_pool, lengths, page_table)
+    context, arrived[2] = lax.optimization_barrier((context, arrived[2]))
     gated = (jax.nn.sigmoid(gate_raw) * context.reshape(req_count, q_local * head_dim)).astype(
         jnp.bfloat16
     )

time: 161 us -> 145 us (0.901)
  local copies, waits for them, and re-layouts: 30.1 us -> 22.8 us
  Pallas kernels: 108 us -> 102 us
    pallas_call x1, Pallas kernels: 25.7 us -> 17.7 us  [merged_norm(): pl.pallas_call(functools.partial(merge_kernel, n, groups), out_shape=(jax...]
    gather x6 -> x0, local copies, waits for them, and re-layouts: 6.2 us -> none  [the longest x5 5.55 us: per_device(): send_pages = page_table[send_rows, :MIGP]]
    mul x3, local copies, waits for them, and re-layouts: 2.77 us -> 0.42 us  [attend(): queries.astype(jnp.float32)[:, :, :, None, :] * which]
    dot_general x1, matrix products: 2.25 us -> 0.5 us  [per_device(): gate_raw = jnp.dot(normed, w_gate_attn, preferred_element_type=jnp.float32)]
    dot_general x1, matrix products: 2.18 us -> 0.47 us  [per_device(): jnp.dot(normed, w_q, preferred_element_type=jnp.float32)]
    unnamed x47 -> x57, local copies, waits for them, and re-layouts: 12.1 us -> 11.4 us
  transfers between devices with their start and end apart: 7 -> 7, of which waited for: 0 -> 0; matrix products, arithmetic and copies ran while one was open for 18% -> 15% of each run, Pallas kernels for 35% -> 34%
where the time goes in v3:
time: 145 us; the launch traced here: 143 us
  Pallas kernels  102 us (70%)
  local copies, waits for them, and re-layouts  22.8 us (16%)
  starting transfers between devices  7.07 us (5%)
  other arithmetic  5.87 us (4%)
  matrix products  4.81 us (3%)
    pallas_call x1, Pallas kernels, mlp(): pl.pallas_call(functools.partial(mlp_kernel, n, groups), out_shape=jax.Sh...  40.8 us
    pallas_call x1, Pallas kernels, attend(): pl.pallas_call(functools.partial(attend_kernel, slots, group, blocks, per...  19.1 us
    pallas_call x1, Pallas kernels, merged_norm(): pl.pallas_call(functools.partial(merge_kernel, n, groups), out_shape=(jax...  17.7 us
    pallas_call x1, Pallas kernels, gathered_norm(): pl.pallas_call(functools.partial(norm_kernel, n), out_shape=jax.ShapeDtyp...  11.5 us
    unnamed x57, local copies, waits for them, and re-layouts  11.4 us
    pallas_call x1, Pallas kernels, pack_blocks(): pl.pallas_call(functools.partial(pack_kernel, count), out_shape=[jax.Shap...  8.36 us
    ppermute x7, starting transfers between devices, per_device(): lax.ppermute(packed[s], 'req', [(i, i ^ s) for i in range(req_groups)])  7.07 us
    pallas_call x1, Pallas kernels, place_blocks(): pl.pallas_call(functools.partial(place_kernel, count), out_shape=(shape,...  4.4 us
  transfers between devices with their start and end apart: 7, of which 0 were waited for; matrix products, arithmetic and copies ran while one was open for 15% of the time, Pallas kernels for 34%

profile of v3, /device:TPU:0, one launch (start us, length us, event | category | flops | bytes accessed | tf_op | source)
XLA Modules:
  0.0 143.4 jit_solution(13573462925367237535)
XLA Ops:
  0.7 0.9 copy.34.page_ref
  1.6 0.9 select_reduce_fusion.1
  3.2 8.4 %pack_blocks.1 = (bf16[2,512,256]{2,1,0:T(8,128)(2,1)S(1)}, bf16[2,512,256]{2,1,0:T(8,128)(2,1)}, bf16[2,512,256]{2,1,0:T(8,128)(2,1)}, bf16[2,512,256]{2,1,0:T(...) custom-call(s32[8]{0:T(128)S(1)} %get-tuple-element.74.send_ref, ...), custom_call_target="tpu_custom_call" | custom-call | tf_op jit(solution)/shard_map/pack_blocks/pallas_call | solution.py:217
  12.6 2.8 %collective-permute-start.1 = (bf16[2,512,256]{2,1,0:T(8,128)(2,1)}, bf16[2,512,256]{2,1,0:T(8,128)(2,1)}, u32[]{:S(2)}, u32[]{:S(2)}) collective-permute-start(bf16[2,512,256]{2,1,0:T(8,128)(2,1)} %get-tuple-element.51), channel_id=1, source_target_pairs={{0,8},{4,12},{8,0},{12,4},{16,24},{20,28},{24,16},{28,20},{1,9},{5... | collective-permute-start | bytes 1572872 | tf_op jit(solution)/shard_map/ppermute | solution.py:549
  15.5 1.3 collective-permute-start.3
  18.5 11.5 %gathered_norm.1 = bf16[64,2048]{1,0:T(8,128)(2,1)} custom-call(bf16[64,512]{1,0:T(8,128)(2,1)} %hidden_ref.1, f32[1,2048]{1,0:T(1,128)} %bitcast.58), custom_call_target="tpu_custom_call" | custom-call | tf_op jit(solution)/shard_map/gathered_norm/pallas_call | solution.py:315
  31.0 2.2 %collective-permute-start.5 = (bf16[2,512,256]{2,1,0:T(8,128)(2,1)}, bf16[2,512,256]{2,1,0:T(8,128)(2,1)}, u32[]{:S(2)}, u32[]{:S(2)}) collective-permute-start(bf16[2,512,256]{2,1,0:T(8,128)(2,1)} %copy-done.16), channel_id=1, source_target_pairs={{0,24},{4,28},{8,16},{12,20},{16,8},{20,12},{24,0},{28,4},{1,25},{... | collective-permute-start | bytes 1572872 | tf_op jit(solution)/shard_map/ppermute | solution.py:549
  33.2 1.6 %convolution_convert_fusion = bf16[64,256]{1,0:T(8,128)(2,1)S(1)} fusion(bf16[64,2048]{1,0:T(8,128)(2,1)} %gathered_norm.1, bf16[2048,256]{1,0:T(8,128)(2,1)} %param.26), kind=kOutput, calls=%fused_computation.11 | convolution fusion | flops 67125248 | bytes 1343488 | tf_op jit(solution)/shard_map/dot_general | solution.py:562
  35.5 2.2 %fusion.14 = f32[64,256]{1,0:T(8,128)} fusion(bf16[64,2048]{1,0:T(8,128)(2,1)} %gathered_norm.1, bf16[2048,256]{1,0:T(8,128)(2,1)} %param.25), kind=kOutput, calls=%fused_computation.56 | convolution fusion | flops 67108864 | bytes 1376256 | tf_op jit(solution)/shard_map/dot_general | solution.py:559
  37.8 0.9 reshape.182
  41.3 0.9 broadcast_in_dim.86
  44.5 0.8 pad.12.q_ref
  45.4 19.1 %attend_pool.1 = f32[64,8,128]{2,1,0:T(8,128)} custom-call(s32[150]{0:T(256)} %select_reduce_fusion.code_ref, s32[64]{0:T(128)} %len_ref.3, f32[64,8,256]{2,1,0:T(8,128)} %pad.12.q_ref, f32[64,8,128]{2,1,0:T(8,128)} %pad.13.k_new_ref, f32[64,8,128]{2,1,0:T(8,128)} %pad.14.v_new_ref, bf16[150,128,256]{2,1,0:T(8,128)(2,1)} %refs_4_.3, ...), custom_call_target="tpu_custom_call" | custom-call | flops 157286400 | bytes 19660800 | tf_op jit(solution)/shard_map/attend_pool/pallas_call | solution.py:152
  64.5 1.0 slice.39
  66.9 2.1 %gather_fusion = bf16[8,512]{1,0:T(8,128)(2,1)} fusion(bf16[64,512]{1,0:T(8,128)(2,1)} %pad_maximum_fusion, s32[1024]{0:T(1024)} %copy-done.24), kind=kCustom, calls=%fused_computation | custom fusion | bytes 16416 | tf_op jit(solution)/shard_map/gather | solution.py:584
  70.5 1.6 %copy-done.3 = bf16[512,2048]{1,0:T(8,128)(2,1)S(1)} copy-done((bf16[512,2048]{1,0:T(8,128)(2,1)S(1)}, bf16[512,2048]{1,0:T(8,128)(2,1)}, u32[]{:S(2)}) %copy-start.3) | copy-done | bytes 2097176
  72.1 17.7 %merged_norm.1 = (bf16[64,512]{1,0:T(8,128)(2,1)S(1)}, bf16[64,2048]{1,0:T(8,128)(2,1)S(1)}, f32[8,8,640]{2,1,0:T(8,128)S(1)}) custom-call(bf16[64,512]{1,0:T(8,128)(2,1)S(1)} %fusion.4.gated_ref, bf16[512,2048]{1,0:T(8,128)(2,1)S(1)} %copy-done.3, bf16[64,512]{1,0:T(8,128)(2,1)S(1)} %copy-done.9, f32[1,2048]{1,0:T(1,128)S(1)} %bitcast.45, ...), custom_call_target="tpu_custom_call" | custom-call | tf_op jit(solution)/shard_map/merged_norm/pallas_call | solution.py:377
  91.8 1.5 %gather_fusion.2 = f32[8,640]{1,0:T(8,128)S(1)} fusion(f32[8,8,640]{2,1,0:T(8,128)} %copy-done.12, s32[8]{0:T(128)S(1)} %fusion.11), kind=kCustom, calls=%fused_computation.2 | custom fusion | bytes 41024 | tf_op jit(solution)/shard_map/gather | solution.py:597
  93.5 1.1 copy-done.5
  94.7 1.1 copy-done.6
  95.8 0.9 copy-done.11
  96.8 0.8 copy-done.14
  97.6 40.8 %mlp_exchange.1 = bf16[64,512]{1,0:T(8,128)(2,1)S(1)} custom-call(bf16[64,2048]{1,0:T(8,128)(2,1)S(1)} %copy-done.11, bf16[192,2048]{1,0:T(8,128)(2,1)S(1)} %bitcast.42, bf16[192,2048]{1,0:T(8,128)(2,1)S(1)} %bitcast.43, bf16[192,2048]{1,0:T(8,128)(2,1)S(1)} %bitcast.44, bf16[64,512]{1,0:T(8,128)(2,1)S(1)} %copy-done.14), custom_call_target="tpu_custom_call" | custom-call | tf_op jit(solution)/shard_map/mlp_exchange/pallas_call | solution.py:483
  138.4 4.4 %place_blocks.1 = (bf16[8,512,256]{2,1,0:T(8,128)(2,1)}, bf16[8,512,256]{2,1,0:T(8,128)(2,1)}) custom-call(s32[8]{0:T(128)S(1)} %iota_xor_fusion.where_ref, s32[8]{0:T(128)S(1)} %fusion.7.len_ref, bf16[8,1,512]{2,1,0:T(2,128)(2,1)S(1)} %copy.40.fresh_ref, bf16[2,512,256]{2,1,0:T(8,128)(2,1)S(1)} %get-tuple-element.63.refs_0_, ...), custom_call_target="tpu_custom_call" | custom-call | tf_op jit(solution)/shard_map/place_blocks/pallas_call | solution.py:248
  (105 shorter events, 15.6 us)
Async XLA Ops:
  0.6 42.3 %copy-start = (bf16[2048,512]{1,0:T(8,128)(2,1)S(1)}, bf16[2048,512]{1,0:T(8,128)(2,1)}, u32[]{:S(2)}) copy-start(bf16[2048,512]{1,0:T(8,128)(2,1)} %param.23) | copy-start | bytes 6291460
  3.2 13.9 %copy-start.23 = (s32[64,32]{0,1:T(8,128)S(1)}, s32[64,32]{0,1:T(8,128)}, u32[]{:S(2)}) copy-start(s32[64,32]{0,1:T(8,128)} %param.31) | copy-start | bytes 24580
  3.2 14.0 %copy-start.2 = (s32[64]{0:T(128)S(1)}, s32[64]{0:T(128)}, u32[]{:S(2)}) copy-start(s32[64]{0:T(128)} %len_ref.3) | copy-start | bytes 772
  12.3 18.7 %collective-permute-start = (bf16[2,512,256]{2,1,0:T(8,128)(2,1)}, bf16[2,512,256]{2,1,0:T(8,128)(2,1)S(1)}, u32[]{:S(2)}, u32[]{:S(2)}) collective-permute-start(bf16[2,512,256]{2,1,0:T(8,128)(2,1)} %get-tuple-element.48), channel_id=1, source_target_pairs={{0,4},{4,0},{8,12},{12,8},{16,20},{20,16},{24,28},{28,24},{1,5},{5... | collective-permute-start | bytes 1572872 | tf_op jit(solution)/shard_map/ppermute | solution.py:549
  12.6 52.9 %collective-permute-start.1 = (bf16[2,512,256]{2,1,0:T(8,128)(2,1)}, bf16[2,512,256]{2,1,0:T(8,128)(2,1)}, u32[]{:S(2)}, u32[]{:S(2)}) collective-permute-start(bf16[2,512,256]{2,1,0:T(8,128)(2,1)} %get-tuple-element.51), channel_id=1, source_target_pairs={{0,8},{4,12},{8,0},{12,4},{16,24},{20,28},{24,16},{28,20},{1,9},{5... | collective-permute-start | bytes 1572872 | tf_op jit(solution)/shard_map/ppermute | solution.py:549
  15.4 78.1 %collective-permute-start.2 = (bf16[2,512,256]{2,1,0:T(8,128)(2,1)}, bf16[2,512,256]{2,1,0:T(8,128)(2,1)}, u32[]{:S(2)}, u32[]{:S(2)}) collective-permute-start(bf16[2,512,256]{2,1,0:T(8,128)(2,1)} %get-tuple-element.53), channel_id=1, source_target_pairs={{0,12},{4,8},{8,4},{12,0},{16,28},{20,24},{24,20},{28,16},{1,13},{... | collective-permute-start | bytes 1572872 | tf_op jit(solution)/shard_map/ppermute | solution.py:549
  15.5 78.0 %collective-permute-start.3 = (bf16[2,512,256]{2,1,0:T(8,128)(2,1)}, bf16[2,512,256]{2,1,0:T(8,128)(2,1)}, u32[]{:S(2)}, u32[]{:S(2)}) collective-permute-start(bf16[2,512,256]{2,1,0:T(8,128)(2,1)} %get-tuple-element.54), channel_id=1, source_target_pairs={{0,16},{4,20},{8,24},{12,28},{16,0},{20,4},{24,8},{28,12},{1,17},{... | collective-permute-start | bytes 1572872 | tf_op jit(solution)/shard_map/ppermute | solution.py:549
  16.9 76.6 %collective-permute-start.4 = (bf16[2,512,256]{2,1,0:T(8,128)(2,1)}, bf16[2,512,256]{2,1,0:T(8,128)(2,1)}, u32[]{:S(2)}, u32[]{:S(2)}) collective-permute-start(bf16[2,512,256]{2,1,0:T(8,128)(2,1)} %get-tuple-element.55), channel_id=1, source_target_pairs={{0,20},{4,16},{8,28},{12,24},{16,4},{20,0},{24,12},{28,8},{1,21},{... | collective-permute-start | bytes 1572872 | tf_op jit(solution)/shard_map/ppermute | solution.py:549
  31.0 11.9 %copy-start.17 = (bf16[64,2048]{1,0:T(8,128)(2,1)S(1)}, bf16[64,2048]{1,0:T(8,128)(2,1)}, u32[]{:S(2)}) copy-start(bf16[64,2048]{1,0:T(8,128)(2,1)} %gathered_norm.1) | copy-start | bytes 786436
  31.0 10.3 %copy-start.7 = (bf16[2,512,256]{2,1,0:T(8,128)(2,1)}, bf16[2,512,256]{2,1,0:T(8,128)(2,1)S(1)}, u32[]{:S(2)}) copy-start(bf16[2,512,256]{2,1,0:T(8,128)(2,1)S(1)} %collective-permute-done.refs_1_) | copy-start | bytes 1572868
  31.0 62.5 %collective-permute-start.5 = (bf16[2,512,256]{2,1,0:T(8,128)(2,1)}, bf16[2,512,256]{2,1,0:T(8,128)(2,1)}, u32[]{:S(2)}, u32[]{:S(2)}) collective-permute-start(bf16[2,512,256]{2,1,0:T(8,128)(2,1)} %copy-done.16), channel_id=1, source_target_pairs={{0,24},{4,28},{8,16},{12,20},{16,8},{20,12},{24,0},{28,4},{1,25},{... | collective-permute-start | bytes 1572872 | tf_op jit(solution)/shard_map/ppermute | solution.py:549
  39.9 3.7 %copy-start.25 = (f32[128]{0:T(128)S(1)}, f32[128]{0:T(128)}, u32[]{:S(2)}) copy-start(f32[128]{0:T(128)} %param.21) | copy-start | bytes 1540
  45.3 20.4 %copy-start.18 = (bf16[64,2048]{1,0:T(8,128)(2,1)S(1)}, bf16[64,2048]{1,0:T(8,128)(2,1)}, u32[]{:S(2)}) copy-start(bf16[64,2048]{1,0:T(8,128)(2,1)} %gathered_norm.1) | copy-start | bytes 786436
  45.3 20.4 %copy-start.19 = (bf16[2048,512]{1,0:T(8,128)(2,1)S(1)}, bf16[2048,512]{1,0:T(8,128)(2,1)}, u32[]{:S(2)}) copy-start(bf16[2048,512]{1,0:T(8,128)(2,1)} %param.24) | copy-start | bytes 6291460
  64.4 1.8 %copy-start.21 = (bf16[64,256]{1,0:T(8,128)(2,1)S(1)}, bf16[64,256]{1,0:T(8,128)(2,1)}, u32[]{:S(2)}) copy-start(bf16[64,256]{1,0:T(8,128)(2,1)} %copy-done.20) | copy-start | bytes 98308
  64.4 1.8 %copy-start.22 = (bf16[8,8,2,128]{3,1,2,0:T(8,128)(2,1)S(1)}, bf16[8,8,2,128]{3,1,2,0:T(8,128)(2,1)}, u32[]{:S(2)}) copy-start(bf16[8,8,2,128]{3,1,2,0:T(8,128)(2,1)} %copy.49) | copy-start | bytes 98308
  64.4 6.0 %copy-start.9 = (bf16[64,512]{1,0:T(8,128)(2,1)S(1)}, bf16[64,512]{1,0:T(8,128)(2,1)}, u32[]{:S(2)}) copy-start(bf16[64,512]{1,0:T(8,128)(2,1)} %hidden_ref.1) | copy-start | bytes 196612
  64.4 6.0 %copy-start.15 = (f32[2048]{0:T(1024)S(1)}, f32[2048]{0:T(1024)}, u32[]{:S(2)}) copy-start(f32[2048]{0:T(1024)} %param.34) | copy-start | bytes 24580
  65.5 28.0 %collective-permute-start.6 = (bf16[2,512,256]{2,1,0:T(8,128)(2,1)}, bf16[2,512,256]{2,1,0:T(8,128)(2,1)}, u32[]{:S(2)}, u32[]{:S(2)}) collective-permute-start(bf16[2,512,256]{2,1,0:T(8,128)(2,1)} %get-tuple-element.57), channel_id=1, source_target_pairs={{0,28},{4,24},{8,20},{12,16},{16,12},{20,8},{24,4},{28,0},{1,29},{... | collective-permute-start | bytes 1572872 | tf_op jit(solution)/shard_map/ppermute | solution.py:549
  65.7 27.8 %copy-start.4 = (bf16[2048,192]{0,1:T(8,128)(2,1)S(1)}, bf16[2048,192]{0,1:T(8,128)(2,1)}, u32[]{:S(2)}) copy-start(bf16[2048,192]{0,1:T(8,128)(2,1)} %param.35) | copy-start | bytes 2359300
  70.5 1.6 %copy-start.3 = (bf16[512,2048]{1,0:T(8,128)(2,1)S(1)}, bf16[512,2048]{1,0:T(8,128)(2,1)}, u32[]{:S(2)}) copy-start(bf16[512,2048]{1,0:T(8,128)(2,1)} %w_ref.1) | copy-start | bytes 6291460
  93.5 1.1 copy-start.5
  94.7 1.1 copy-start.6
  97.6 40.8 %copy-start.8 = (bf16[2,512,256]{2,1,0:T(8,128)(2,1)S(1)}, bf16[2,512,256]{2,1,0:T(8,128)(2,1)}, u32[]{:S(2)}) copy-start(bf16[2,512,256]{2,1,0:T(8,128)(2,1)} %copy-done.7) | copy-start | bytes 1572868
  (9 other events, 6.7 us)
